TPU v7x, 512 devices: a whole 4x8x8 slice. The times are simulated.
512 devices in a mesh: band: 16 (over z, core), tile: 32 (over x, y).
Axes of the slice: x: 4, y: 8, z: 8, core: 2. Of those that a mesh axis runs over, the one named last changes fastest.
Arguments:
- displacement: float32 [3, 128, 512, 512], P(None, 'band', 'tile'), may hold values from -3 to 3
- old_mass: float32 [262144, 128], P(('band', 'tile')), may hold values from 0.5 to 2
- old_momentum: float32 [262144, 3, 128], P(('band', 'tile')), may hold values from -6 to 6
- intersection_fraction: float32 [262144, 128], P(('band', 'tile')), may hold values from 0.1 to 0.9
- entry_order: int32 [512, 1024], P(('band', 'tile')), may hold values from 0 to 1023, each once within a row
- target_owner: int32 [524288, 1], P(('band', 'tile')), may hold values from 0 to 31; in each aligned block of 1024 rows (0 to 1023, 1024 to 2047, ...) at most 40 rows name the same one
- target_block: int32 [524288], P(('band', 'tile')), may hold values from 0 to 511
- kept_mass: float32 [128, 512, 512], P('band', 'tile'), may hold values from 0.5 to 2
- kept_momentum: float32 [3, 128, 512, 512], P(None, 'band', 'tile'), may hold values from -6 to 6
- surface_panels: float32 [2048, 3, 128], P(('band', 'tile')), may hold values from -6 to 6
- panel_ids: int32 [16, 512, 4], P('band', 'tile'), may hold values from 0 to 127
- contact_flags: int32 [16, 512, 4], P('band', 'tile'), may hold values 0 or 1
Outputs:
- regridded: float32 [3, 128, 512, 512], P(None, 'band', 'tile')
- velocity: float32 [3, 128, 512, 512], P(None, 'band', 'tile')
Inputs may be any that keep to these rules, and one draw needn't show every extreme that they name: `entry_order`: each device's row is a permutation of 0 to 1023. `target_owner`: among the 1024 entries of one device no owner is named more than 40 times, a bound that some block reaches.
All inputs are finite; a program needn't handle non-finite values. No bound on the sum of `contact_flags` on one device may be relied on, other than what follows from the above.
Results may differ from a plain program's by a relative error of at most 0.0003.
Values sent between devices are 32-bit elements; how exact they have to be, the bound alone decides.
A program may use at most 64 MiB of HBM per device.

v0:
```python
import jax
import jax.numpy as jnp
from jax import lax
from jax.sharding import PartitionSpec as P

ITERS_W = 2


relax_factor = 0.8
cell_fraction = 0.1
strain_eps = 0.05
rate_power = -0.4
penalty_factor = 0.5


def extended(x, sides, width):
    for axis, dim in sides:
        peers, length = (lax.axis_size(axis), x.shape[dim])
        up = [(i, (i + 1) % peers) for i in range(peers - 1)]
        down = [(j, i) for i, j in up]
        last = lax.slice_in_dim(x, length - width, length, axis=dim)
        initial = lax.slice_in_dim(x, 0, width, axis=dim)
        before = lax.ppermute(last, axis, up)
        after = lax.ppermute(initial, axis, down)
        x = jnp.concatenate([before, x, after], axis=dim)
    return x


def ahead(grid_field, dimension):
    padding = [(0, 0)] * grid_field.ndim
    padding[dimension] = (0, 1)
    extent = grid_field.shape[dimension]
    return lax.slice_in_dim(jnp.pad(grid_field, padding), 1, extent + 1, axis=dimension)


def behind(grid_field, dimension):
    padding = [(0, 0)] * grid_field.ndim
    padding[dimension] = (1, 0)
    extent = grid_field.shape[dimension]
    return lax.slice_in_dim(jnp.pad(grid_field, padding), 0, extent, axis=dimension)


def widen(grid_field, margin):
    padding = [(0, 0)] * (grid_field.ndim - 1) + [(margin, margin)]
    return jnp.pad(grid_field, padding)


def crop(grid_field, margin):
    return grid_field[..., margin:-margin, margin:-margin, margin:-margin]


def inside_mask(margin, layers, across, length):
    band_rows = lax.axis_index("band") * layers + jnp.arange(-margin, layers + margin)
    in_band = (band_rows >= 0) & (band_rows < layers * lax.axis_size("band"))
    tile_rows = lax.axis_index("tile") * across + jnp.arange(-margin, across + margin)
    in_tile = (tile_rows >= 0) & (tile_rows < across * lax.axis_size("tile"))
    lane_rows = jnp.arange(-margin, length + margin)
    in_lane = (lane_rows >= 0) & (lane_rows < length)
    return (in_band[:, None, None] & in_tile[None, :, None] & in_lane[None, None, :]).astype(
        jnp.float32
    )


def smooth(padded):
    neighbours = jnp.zeros_like(padded)
    for dimension in (1, 2, 3):
        neighbours = neighbours + ahead(padded, dimension) + behind(padded, dimension)
    return padded + relax_factor * (neighbours / 6.0 - padded)


def volume_of(padded):
    stretch = jnp.zeros_like(padded[0])
    for component in range(3):
        stretch = stretch + 0.5 * (
            ahead(padded[component], component) - behind(padded[component], component)
        )
    return 1.0 + cell_fraction * stretch


def viscosity_of(padded):
    squares = jnp.zeros_like(padded[0])
    for component in range(3):
        for dimension in range(3):
            change = ahead(padded[component], dimension) - padded[component]
            squares = squares + change * change
    return (strain_eps + squares) ** rate_power


def pressure_of(padded):
    divergence = jnp.zeros_like(padded[0])
    for component in range(3):
        divergence = divergence + (padded[component] - behind(padded[component], component))
    return -penalty_factor * divergence


def update(padded_speed, padded_visc, pressure, margin, density, traction):
    face_sum = jnp.zeros_like(padded_visc)
    fluxes = [jnp.zeros_like(padded_visc) for component in range(3)]
    for dimension in range(3):
        forward_face = 0.5 * (padded_visc + ahead(padded_visc, dimension))
        backward_face = 0.5 * (padded_visc + behind(padded_visc, dimension))
        face_sum = face_sum + forward_face + backward_face
        for component in range(3):
            fluxes[component] = (
                fluxes[component]
                + forward_face * ahead(padded_speed[component], dimension)
                + backward_face * behind(padded_speed[component], dimension)
            )
    denominator = crop(face_sum, margin) + density
    results = []
    for component in range(3):
        gradient = crop(ahead(pressure, component) - pressure, margin)
        speed_here = crop(padded_speed[component], margin)
        numerator = (
            crop(fluxes[component], margin)
            - gradient
            + traction[component][None]
            + density * speed_here
        )
        results.append(numerator / denominator)
    return jnp.stack(results)


def shards(
    displacement,
    old_mass,
    old_momentum,
    intersection_fraction,
    entry_order,
    target_owner,
    target_block,
    kept_mass,
    kept_momentum,
    surface_panels,
    panel_ids,
    contact_flags,
):
    layers, across, length = (displacement.shape[1], displacement.shape[2], displacement.shape[3])
    blocks_local = old_mass.shape[0]
    owners = target_owner[:, 0]
    n_tile = lax.axis_size("tile")
    entries = owners.shape[0]
    capacity = max(2, (5 * entries + 4 * n_tile - 1) // (4 * n_tile))
    chosen = (owners[:, None] == jnp.arange(n_tile, dtype=jnp.int32)[None, :]).astype(jnp.int32)
    before = jnp.cumsum(chosen, axis=0) - chosen
    slot_index = jnp.sum(before * chosen, axis=1)
    position = owners * capacity + slot_index
    order_row = entry_order[0]
    source = order_row // 2
    fraction = intersection_fraction[source]
    weights = jnp.where((order_row % 2 == 0)[:, None], fraction, 1.0 - fraction)
    buffer_mass = (
        jnp.zeros((n_tile * capacity, 128), jnp.float32)
        .at[position]
        .set(weights * old_mass[source])
    )
    buffer_momentum = (
        jnp.zeros((n_tile * capacity, 3, 128), jnp.float32)
        .at[position]
        .set(weights[:, None, :] * old_momentum[source])
    )
    buffer_block = jnp.full((n_tile * capacity,), -1, jnp.int32).at[position].set(target_block)
    received_mass, received_momentum, received_block = (
        lax.all_to_all(
            buffer_mass.reshape(n_tile, capacity, 128),
            "tile",
            split_axis=0,
            concat_axis=0,
            tiled=True,
        ),
        lax.all_to_all(
            buffer_momentum.reshape(n_tile, capacity, 3, 128),
            "tile",
            split_axis=0,
            concat_axis=0,
            tiled=True,
        ),
        lax.all_to_all(
            buffer_block.reshape(n_tile, capacity), "tile", split_axis=0, concat_axis=0, tiled=True
        ),
    )
    regridded = displacement
    for sweep_index in range(ITERS_W):
        padded = widen(extended(regridded, (("band", 1), ("tile", 2)), 1), 1)
        regridded = crop(smooth(padded), 1)
    padded = widen(extended(regridded, (("band", 1), ("tile", 2)), 1), 1)
    volume = crop(volume_of(padded), 1)
    gathered = lax.all_gather(surface_panels, "tile", axis=0, tiled=True)
    picked = gathered[panel_ids[0]] * contact_flags[0].astype(jnp.float32)[:, :, None, None]
    traction = picked.transpose(2, 0, 1, 3).reshape(3, across, length)
    flat_block = received_block.reshape(-1)
    selector = (jnp.arange(blocks_local, dtype=jnp.int32)[:, None] == flat_block[None, :]).astype(
        jnp.float32
    )
    incoming_mass = jnp.dot(
        selector,
        received_mass.reshape(-1, 128),
        precision=lax.Precision.HIGHEST,
        preferred_element_type=jnp.float32,
    )
    incoming_momentum = jnp.einsum(
        "br,rcl->cbl",
        selector,
        received_momentum.reshape(-1, 3, 128),
        precision=lax.Precision.HIGHEST,
    )
    mass = kept_mass + incoming_mass.reshape(layers, across, length)
    momentum = kept_momentum + incoming_momentum.reshape(3, layers, across, length)
    speed = momentum / mass[None]
    density = mass / volume
    padded_speed = widen(extended(speed, (("band", 1), ("tile", 2)), 1), 1)
    viscous_local = crop(viscosity_of(padded_speed), 1)
    padded_visc = widen(extended(viscous_local, (("band", 0), ("tile", 1)), 1), 1)
    pressure = pressure_of(padded_speed) * inside_mask(1, layers, across, length)
    velocity = update(padded_speed, padded_visc, pressure, 1, density, traction)
    return (regridded, velocity)


def solution(mesh):
    return jax.shard_map(
        shards,
        mesh=mesh,
        in_specs=(
            P(None, "band", "tile", None),
            P(("band", "tile"), None),
            P(("band", "tile"), None, None),
            P(("band", "tile"), None),
            P(("band", "tile"), None),
            P(("band", "tile"), None),
            P(("band", "tile")),
            P("band", "tile", None),
            P(None, "band", "tile", None),
            P(("band", "tile"), None, None),
            P("band", "tile", None),
            P("band", "tile", None),
        ),
        out_specs=(P(None, "band", "tile", None), P(None, "band", "tile", None)),
        check_vma=False,
    )
```

profile of v0, /device:TPU:249, one launch (start us, length us, event | category | flops | bytes accessed | tf_op | source)
XLA Modules:
  0.0 338.3 jit_solution(12221945368316024216)
XLA Ops:
  1.4 9.0 %reduce-window.6 = s32[32,8,128]{2,1,0:T(8,128)S(1)} reduce-window(s32[32,8,128]{2,1,0:T(8,128)S(1)} %fusion.74, s32[]{:T(128)} %constant.31.clone.1), window={size=1x1x128 pad=0_0x0_0x127_0}, to_apply=%region_0.0 | reduce-window | flops 4161536 | bytes 262148 | tf_op jit(solution)/shard_map/reduce-window
  12.4 4.5 %scatter_custom_fusion.1 = s32[1280]{0:T(1024)S(1)} fusion(s32[1024]{0:T(1024)S(1)} %bitcast.107, s32[1024]{0:T(1024)} %param.18, s32[]{:T(128)} %constant.36.clone.1), kind=kCustom, calls=%fused_computation.222 | custom fusion | bytes 5632 | tf_op jit(solution)/shard_map/scatter | solution.py:162
  17.5 8.9 %all-to-all-start.1 = ((s32[32,1,40]{2,1,0:T(1,128)}), s32[32,1,40]{2,1,0:T(1,128)S(1)}, u32[]{:S(2)}, u32[]{:S(2)}) async-start(s32[32,1,40]{2,1,0:T(1,128)} %all_to_all.13), calls=%async_computation.1 | async-start | bytes 32768 | tf_op jit(solution)/shard_map/all_to_all | solution.py:178
  26.5 1.6 fusion.88
  28.1 3.1 collective-permute-start.1
  31.3 5.1 %collective-permute-start = (f32[3,1,16,512]{3,2,1,0:T(8,128)}, f32[3,1,16,512]{3,2,1,0:T(8,128)}, u32[]{:S(2)}, u32[]{:S(2)}) collective-permute-start(f32[3,1,16,512]{3,2,1,0:T(8,128)} %get-tuple-element.30), channel_id=1, source_target_pairs={{0,32},{32,64},{64,96},{96,128},{128,160},{160,192},{192,224},{224... | collective-permute-start | bytes 294920 | tf_op jit(solution)/shard_map/ppermute | solution.py:23
  38.6 2.8 gather_fusion
  41.4 7.2 %scatter_custom_fusion.2 = f32[1280,128]{1,0:T(8,128)} fusion(s32[1024]{0:T(1024)S(1)} %bitcast.108, f32[]{:T(128)} %constant.27.clone.1, f32[512,128]{1,0:T(8,128)S(1)} %copy-done.9, s32[1024]{0:T(1024)S(1)} %broadcast_clamp_fusion, f32[1024,128]{1,0:T(8,128)S(1)} %gather_fusion, pred[1024]{0:T(1024)(128)(4,1)S(1)} %fusion.76), kind=kCustom, calls=%fused_computation.109 | custom fusion | flops 393216 | bytes 1446916 | tf_op jit(solution)/shard_map/scatter | solution.py:155
  48.6 9.3 %all-to-all-start.2 = ((f32[32,40,128]{2,1,0:T(8,128)}), f32[32,40,128]{2,1,0:T(8,128)}, u32[]{:S(2)}, u32[]{:S(2)}) async-start(f32[32,40,128]{2,1,0:T(8,128)} %bitcast.13), calls=%async_computation.2 | async-start | bytes 1310720 | tf_op jit(solution)/shard_map/all_to_all | solution.py:164
  58.2 3.9 %gather_fusion.1 = f32[1024,3,128]{2,0,1:T(8,128)S(1)} fusion(f32[512,3,128]{2,0,1:T(8,128)S(1)} %copy-done, s32[1024]{0:T(1024)S(1)} %broadcast_clamp_fusion), kind=kCustom, calls=%fused_computation.1 | custom fusion | bytes 3149824 | tf_op jit(solution)/shard_map/gather | solution.py:160
  62.0 41.5 %all_gather.3 = f32[128,3,128]{2,1,0:T(4,128)S(1)} all-gather(f32[4,3,128]{2,1,0:T(4,128)S(1)} %copy.33), channel_id=1, replica_groups=mesh['band'=16,'tile'=32] {'tile'}, dimensions={0}, use_global_device_ids=true | all-gather | bytes 202752 | tf_op jit(solution)/shard_map/all_gather | solution.py:188
  105.8 3.8 %copy.27 = f32[1024,3,128]{2,1,0:T(4,128)} copy(f32[1024,3,128]{2,0,1:T(8,128)} %broadcast_multiply_fusion) | data formatting | bytes 3145728 | tf_op jit(solution)/shard_map/mul | solution.py:160
  110.4 62.2 %scatter_fusion = f32[1280,3,128]{2,1,0:T(4,128)S(1)} fusion(f32[1280,3,128]{2,1,0:T(4,128)S(1)} %broadcast_in_dim.14, s32[1024]{0:T(1024)S(1)} %bitcast.109, f32[1024,3,128]{2,1,0:T(4,128)} %copy.27), kind=kCustom, calls=%fused_computation.4 | custom fusion | bytes 4722688 | tf_op jit(solution)/shard_map/scatter | solution.py:160
  175.5 7.8 %all-to-all-start = ((f32[32,40,3,128]{3,1,2,0:T(8,128)}), f32[32,40,3,128]{3,1,2,0:T(8,128)S(1)}, u32[]{:S(2)}, u32[]{:S(2)}) async-start(f32[32,40,3,128]{3,1,2,0:T(8,128)} %copy.29), calls=%async_computation | async-start | bytes 3932160 | tf_op jit(solution)/shard_map/all_to_all | solution.py:171
  184.4 1.6 constant_dynamic-update-slice_fusion
  187.2 3.1 collective-permute-start.2
  190.3 2.4 collective-permute-start.3
  192.7 24.5 %collective-permute-done.2 = f32[3,10,1,512]{3,2,1,0:T(1,128)S(1)} collective-permute-done((f32[3,10,1,512]{3,2,1,0:T(1,128)S(1)}, f32[3,10,1,512]{3,2,1,0:T(1,128)S(1)}, u32[]{:S(2)}, u32[]{:S(2)}) %collective-permute-start.2) | collective-permute-done | bytes 61472 | tf_op jit(solution)/shard_map/ppermute | solution.py:23
  218.3 2.2 select_maximum_fusion.12
  220.5 1.6 fusion.12
  222.2 16.2 %collective-permute-start.4 = (f32[3,1,16,512]{3,2,1,0:T(8,128)S(1)}, f32[3,1,16,512]{3,2,1,0:T(8,128)S(1)}, u32[]{:S(2)}, u32[]{:S(2)}) collective-permute-start(f32[3,1,16,512]{3,2,1,0:T(8,128)S(1)} %get-tuple-element.17), channel_id=1, source_target_pairs={{0,32},{32,64},{64,96},{96,128},{128,160},{160,192},{192,224},{224... | collective-permute-start | bytes 294920 | tf_op jit(solution)/shard_map/ppermute | solution.py:23
  238.4 1.9 collective-permute-start.5
  240.7 4.9 %collective-permute-done.5 = f32[3,1,16,512]{3,2,1,0:T(8,128)S(1)} collective-permute-done((f32[3,1,16,512]{3,2,1,0:T(8,128)S(1)}, f32[3,1,16,512]{3,2,1,0:T(8,128)S(1)}, u32[]{:S(2)}, u32[]{:S(2)}) %collective-permute-start.5) | collective-permute-done | bytes 98336 | tf_op jit(solution)/shard_map/ppermute | solution.py:24
  245.6 4.6 %collective-permute-start.6 = (f32[3,10,1,512]{3,2,1,0:T(1,128)S(1)}, f32[3,10,1,512]{3,2,1,0:T(1,128)S(1)}, u32[]{:S(2)}, u32[]{:S(2)}) collective-permute-start(f32[3,10,1,512]{3,2,1,0:T(1,128)S(1)} %get-tuple-element.23), channel_id=1, source_target_pairs={{0,1},{1,2},{2,3},{3,4},{4,5},{5,6},{6,7},{7,8},{8,9},{9,10},{10,1... | collective-permute-start | bytes 184328 | tf_op jit(solution)/shard_map/ppermute | solution.py:23
  250.3 1.9 collective-permute-start.7
  252.9 4.5 %collective-permute-done.7 = f32[3,10,1,512]{3,2,1,0:T(1,128)S(1)} collective-permute-done((f32[3,10,1,512]{3,2,1,0:T(1,128)S(1)}, f32[3,10,1,512]{3,2,1,0:T(1,128)S(1)}, u32[]{:S(2)}, u32[]{:S(2)}) %collective-permute-start.7) | collective-permute-done | bytes 61472 | tf_op jit(solution)/shard_map/ppermute | solution.py:24
  260.1 3.3 collective-permute-start.16
  263.3 1.9 collective-permute-start.17
  265.9 4.6 %collective-permute-done.17 = f32[3,1,16,512]{3,2,1,0:T(8,128)S(1)} collective-permute-done((f32[3,1,16,512]{3,2,1,0:T(8,128)S(1)}, f32[3,1,16,512]{3,2,1,0:T(8,128)S(1)}, u32[]{:S(2)}, u32[]{:S(2)}) %collective-permute-start.17) | collective-permute-done | bytes 98336 | tf_op jit(solution)/shard_map/ppermute | solution.py:24
  270.6 1.9 collective-permute-start.18
  272.5 3.4 collective-permute-start.19
  277.2 2.4 collective-permute-done.19
  281.8 2.5 fusion
  285.2 3.4 %fusion.25 = f32[3,512,128]{1,2,0:T(8,128)S(1)} fusion(f32[1280,3,128]{2,0,1:T(8,128)S(1)} %bitcast.92, s32[1280]{0:T(1024)S(1)} %eq.59), kind=kOutput, calls=%fused_computation.52 | convolution fusion | flops 3020554240 | bytes 2757632 | tf_op jit(solution)/shard_map/br,rcl->cbl/dot_general | solution.py:201
  291.0 3.0 collective-permute-start.8
  293.9 2.1 collective-permute-start.9
  296.5 4.6 %collective-permute-done.9 = f32[3,1,16,512]{3,2,1,0:T(8,128)S(1)} collective-permute-done((f32[3,1,16,512]{3,2,1,0:T(8,128)S(1)}, f32[3,1,16,512]{3,2,1,0:T(8,128)S(1)}, u32[]{:S(2)}, u32[]{:S(2)}) %collective-permute-start.9) | collective-permute-done | bytes 98336 | tf_op jit(solution)/shard_map/ppermute | solution.py:24
  301.2 1.9 collective-permute-start.10
  303.1 3.4 collective-permute-start.11
  306.6 3.6 %collective-permute-done.11 = f32[3,10,1,512]{3,2,1,0:T(1,128)S(1)} collective-permute-done((f32[3,10,1,512]{3,2,1,0:T(1,128)S(1)}, f32[3,10,1,512]{3,2,1,0:T(1,128)S(1)}, u32[]{:S(2)}, u32[]{:S(2)}) %collective-permute-start.11) | collective-permute-done | bytes 61472 | tf_op jit(solution)/shard_map/ppermute | solution.py:24
  311.9 1.7 add_power_fusion
  313.7 3.0 collective-permute-start.12
  316.7 1.9 collective-permute-start.13
  319.7 3.4 %collective-permute-done.13 = f32[1,16,512]{2,1,0:T(8,128)S(1)} collective-permute-done((f32[1,16,512]{2,1,0:T(8,128)S(1)}, f32[1,16,512]{2,1,0:T(8,128)S(1)}, u32[]{:S(2)}, u32[]{:S(2)}) %collective-permute-start.13) | collective-permute-done | bytes 32800 | tf_op jit(solution)/shard_map/ppermute | solution.py:24
  323.1 1.9 collective-permute-start.14
  325.1 3.4 collective-permute-start.15
  329.1 2.6 collective-permute-done.15
  332.5 2.0 fusion.58
  (116 shorter events, 35.1 us)
Async XLA Ops:
  0.6 57.5 %copy-start = (f32[512,3,128]{2,0,1:T(8,128)S(1)}, f32[512,3,128]{2,0,1:T(8,128)}, u32[]{:S(2)}) copy-start(f32[512,3,128]{2,0,1:T(8,128)} %param.14) | copy-start | bytes 2359300
  0.6 37.9 %copy-start.2 = (f32[512,128]{1,0:T(8,128)S(1)}, f32[512,128]{1,0:T(8,128)}, u32[]{:S(2)}) copy-start(f32[512,128]{1,0:T(8,128)} %param.15) | copy-start | bytes 786436
  12.3 29.0 %copy-start.10 = (s32[1024,1]{0,1:T(1,128)}, s32[1024,1]{0,1:T(1,128)S(1)}, u32[]{:S(2)}) copy-start(s32[1024,1]{0,1:T(1,128)S(1)} %compare_select_fusion.1) | copy-start | bytes 12292
  17.5 31.1 %all-to-all-start.1 = ((s32[32,1,40]{2,1,0:T(1,128)}), s32[32,1,40]{2,1,0:T(1,128)S(1)}, u32[]{:S(2)}, u32[]{:S(2)}) async-start(s32[32,1,40]{2,1,0:T(1,128)} %all_to_all.13), calls=%async_computation.1 | async-start | bytes 32768 | tf_op jit(solution)/shard_map/all_to_all | solution.py:178
  28.1 156.3 %collective-permute-start.1 = (f32[3,1,16,512]{3,2,1,0:T(8,128)}, f32[3,1,16,512]{3,2,1,0:T(8,128)}, u32[]{:S(2)}, u32[]{:S(2)}) collective-permute-start(f32[3,1,16,512]{3,2,1,0:T(8,128)} %get-tuple-element.29), channel_id=1, source_target_pairs={{32,0},{64,32},{96,64},{128,96},{160,128},{192,160},{224,192},{256... | collective-permute-start | bytes 294920 | tf_op jit(solution)/shard_map/ppermute | solution.py:24
  31.3 142.7 %collective-permute-start = (f32[3,1,16,512]{3,2,1,0:T(8,128)}, f32[3,1,16,512]{3,2,1,0:T(8,128)}, u32[]{:S(2)}, u32[]{:S(2)}) collective-permute-start(f32[3,1,16,512]{3,2,1,0:T(8,128)} %get-tuple-element.30), channel_id=1, source_target_pairs={{0,32},{32,64},{64,96},{96,128},{128,160},{160,192},{192,224},{224... | collective-permute-start | bytes 294920 | tf_op jit(solution)/shard_map/ppermute | solution.py:23
  38.6 2.8 copy-start.9
  41.4 16.5 %copy-start.14 = (s32[1,16,4]{1,2,0:T(4,128)S(1)}, s32[1,16,4]{1,2,0:T(4,128)}, u32[]{:S(2)}) copy-start(s32[1,16,4]{1,2,0:T(4,128)} %param.22) | copy-start | bytes 772
  41.4 16.7 %copy-start.13 = (f32[4,3,128]{2,0,1:T(4,128)S(1)}, f32[4,3,128]{2,0,1:T(4,128)}, u32[]{:S(2)}) copy-start(f32[4,3,128]{2,0,1:T(4,128)} %param.21) | copy-start | bytes 18436
  48.6 126.9 %all-to-all-start.2 = ((f32[32,40,128]{2,1,0:T(8,128)}), f32[32,40,128]{2,1,0:T(8,128)}, u32[]{:S(2)}, u32[]{:S(2)}) async-start(f32[32,40,128]{2,1,0:T(8,128)} %bitcast.13), calls=%async_computation.2 | async-start | bytes 1310720 | tf_op jit(solution)/shard_map/all_to_all | solution.py:164
  109.7 0.7 copy-start.11
  175.5 7.9 %copy-start.7 = (f32[3,8,16,512]{3,2,1,0:T(8,128)S(1)}, f32[3,8,16,512]{3,2,1,0:T(8,128)}, u32[]{:S(2)}) copy-start(f32[3,8,16,512]{3,2,1,0:T(8,128)} %param.12) | copy-start | bytes 2359300
  175.5 109.6 %all-to-all-start = ((f32[32,40,3,128]{3,1,2,0:T(8,128)}), f32[32,40,3,128]{3,1,2,0:T(8,128)S(1)}, u32[]{:S(2)}, u32[]{:S(2)}) async-start(f32[32,40,3,128]{3,1,2,0:T(8,128)} %copy.29), calls=%async_computation | async-start | bytes 3932160 | tf_op jit(solution)/shard_map/all_to_all | solution.py:171
  187.2 30.0 %collective-permute-start.2 = (f32[3,10,1,512]{3,2,1,0:T(1,128)S(1)}, f32[3,10,1,512]{3,2,1,0:T(1,128)S(1)}, u32[]{:S(2)}, u32[]{:S(2)}) collective-permute-start(f32[3,10,1,512]{3,2,1,0:T(1,128)S(1)} %get-tuple-element.25), channel_id=1, source_target_pairs={{0,1},{1,2},{2,3},{3,4},{4,5},{5,6},{6,7},{7,8},{8,9},{9,10},{10,1... | collective-permute-start | bytes 184328 | tf_op jit(solution)/shard_map/ppermute | solution.py:23
  190.3 28.0 %collective-permute-start.3 = (f32[3,10,1,512]{3,2,1,0:T(1,128)S(1)}, f32[3,10,1,512]{3,2,1,0:T(1,128)S(1)}, u32[]{:S(2)}, u32[]{:S(2)}) collective-permute-start(f32[3,10,1,512]{3,2,1,0:T(1,128)S(1)} %get-tuple-element.26), channel_id=1, source_target_pairs={{1,0},{2,1},{3,2},{4,3},{5,4},{6,5},{7,6},{8,7},{9,8},{10,9},{11,1... | collective-permute-start | bytes 184328 | tf_op jit(solution)/shard_map/ppermute | solution.py:24
  222.2 18.5 %collective-permute-start.4 = (f32[3,1,16,512]{3,2,1,0:T(8,128)S(1)}, f32[3,1,16,512]{3,2,1,0:T(8,128)S(1)}, u32[]{:S(2)}, u32[]{:S(2)}) collective-permute-start(f32[3,1,16,512]{3,2,1,0:T(8,128)S(1)} %get-tuple-element.17), channel_id=1, source_target_pairs={{0,32},{32,64},{64,96},{96,128},{128,160},{160,192},{192,224},{224... | collective-permute-start | bytes 294920 | tf_op jit(solution)/shard_map/ppermute | solution.py:23
  238.4 7.1 %collective-permute-start.5 = (f32[3,1,16,512]{3,2,1,0:T(8,128)S(1)}, f32[3,1,16,512]{3,2,1,0:T(8,128)S(1)}, u32[]{:S(2)}, u32[]{:S(2)}) collective-permute-start(f32[3,1,16,512]{3,2,1,0:T(8,128)S(1)} %get-tuple-element.18), channel_id=1, source_target_pairs={{32,0},{64,32},{96,64},{128,96},{160,128},{192,160},{224,192},{256... | collective-permute-start | bytes 294920 | tf_op jit(solution)/shard_map/ppermute | solution.py:24
  245.6 7.2 %collective-permute-start.6 = (f32[3,10,1,512]{3,2,1,0:T(1,128)S(1)}, f32[3,10,1,512]{3,2,1,0:T(1,128)S(1)}, u32[]{:S(2)}, u32[]{:S(2)}) collective-permute-start(f32[3,10,1,512]{3,2,1,0:T(1,128)S(1)} %get-tuple-element.23), channel_id=1, source_target_pairs={{0,1},{1,2},{2,3},{3,4},{4,5},{5,6},{6,7},{7,8},{8,9},{9,10},{10,1... | collective-permute-start | bytes 184328 | tf_op jit(solution)/shard_map/ppermute | solution.py:23
  250.3 7.1 %collective-permute-start.7 = (f32[3,10,1,512]{3,2,1,0:T(1,128)S(1)}, f32[3,10,1,512]{3,2,1,0:T(1,128)S(1)}, u32[]{:S(2)}, u32[]{:S(2)}) collective-permute-start(f32[3,10,1,512]{3,2,1,0:T(1,128)S(1)} %get-tuple-element.24), channel_id=1, source_target_pairs={{1,0},{2,1},{3,2},{4,3},{5,4},{6,5},{7,6},{8,7},{9,8},{10,9},{11,1... | collective-permute-start | bytes 184328 | tf_op jit(solution)/shard_map/ppermute | solution.py:24
  260.1 5.8 %collective-permute-start.16 = (f32[3,1,16,512]{3,2,1,0:T(8,128)S(1)}, f32[3,1,16,512]{3,2,1,0:T(8,128)S(1)}, u32[]{:S(2)}, u32[]{:S(2)}) collective-permute-start(f32[3,1,16,512]{3,2,1,0:T(8,128)S(1)} %get-tuple-element.10), channel_id=1, source_target_pairs={{0,32},{32,64},{64,96},{96,128},{128,160},{160,192},{192,224},{224... | collective-permute-start | bytes 294920 | tf_op jit(solution)/shard_map/ppermute | solution.py:23
  263.3 7.1 %collective-permute-start.17 = (f32[3,1,16,512]{3,2,1,0:T(8,128)S(1)}, f32[3,1,16,512]{3,2,1,0:T(8,128)S(1)}, u32[]{:S(2)}, u32[]{:S(2)}) collective-permute-start(f32[3,1,16,512]{3,2,1,0:T(8,128)S(1)} %get-tuple-element.11), channel_id=1, source_target_pairs={{32,0},{64,32},{96,64},{128,96},{160,128},{192,160},{224,192},{256... | collective-permute-start | bytes 294920 | tf_op jit(solution)/shard_map/ppermute | solution.py:24
  265.9 14.7 %copy-start.3 = (f32[3,8,16,512]{3,2,1,0:T(8,128)}, f32[3,8,16,512]{3,2,1,0:T(8,128)S(1)}, u32[]{:S(2)}) copy-start(f32[3,8,16,512]{3,2,1,0:T(8,128)S(1)} %slice.439) | copy-start | bytes 2359300
  270.6 6.6 %collective-permute-start.18 = (f32[3,10,1,512]{3,2,1,0:T(1,128)S(1)}, f32[3,10,1,512]{3,2,1,0:T(1,128)S(1)}, u32[]{:S(2)}, u32[]{:S(2)}) collective-permute-start(f32[3,10,1,512]{3,2,1,0:T(1,128)S(1)} %get-tuple-element.19), channel_id=1, source_target_pairs={{0,1},{1,2},{2,3},{3,4},{4,5},{5,6},{6,7},{7,8},{8,9},{9,10},{10,1... | collective-permute-start | bytes 184328 | tf_op jit(solution)/shard_map/ppermute | solution.py:23
  272.5 7.1 %collective-permute-start.19 = (f32[3,10,1,512]{3,2,1,0:T(1,128)S(1)}, f32[3,10,1,512]{3,2,1,0:T(1,128)S(1)}, u32[]{:S(2)}, u32[]{:S(2)}) collective-permute-start(f32[3,10,1,512]{3,2,1,0:T(1,128)S(1)} %get-tuple-element.20), channel_id=1, source_target_pairs={{1,0},{2,1},{3,2},{4,3},{5,4},{6,5},{7,6},{8,7},{9,8},{10,9},{11,1... | collective-permute-start | bytes 184328 | tf_op jit(solution)/shard_map/ppermute | solution.py:24
  281.8 2.5 copy-start.8
  288.6 1.0 copy-start.6
  289.6 6.5 %copy-start.4 = (f32[10,18,514]{2,1,0:T(8,128)S(1)}, f32[10,18,514]{2,1,0:T(8,128)}, u32[]{:S(2)}) copy-start(f32[10,18,514]{2,1,0:T(8,128)} %get-tuple-element.9) | copy-start | bytes 1110244
  291.0 5.6 %collective-permute-start.8 = (f32[3,1,16,512]{3,2,1,0:T(8,128)S(1)}, f32[3,1,16,512]{3,2,1,0:T(8,128)S(1)}, u32[]{:S(2)}, u32[]{:S(2)}) collective-permute-start(f32[3,1,16,512]{3,2,1,0:T(8,128)S(1)} %get-tuple-element.27), channel_id=1, source_target_pairs={{0,32},{32,64},{64,96},{96,128},{128,160},{160,192},{192,224},{224... | collective-permute-start | bytes 294920 | tf_op jit(solution)/shard_map/ppermute | solution.py:23
  293.9 7.1 %collective-permute-start.9 = (f32[3,1,16,512]{3,2,1,0:T(8,128)S(1)}, f32[3,1,16,512]{3,2,1,0:T(8,128)S(1)}, u32[]{:S(2)}, u32[]{:S(2)}) collective-permute-start(f32[3,1,16,512]{3,2,1,0:T(8,128)S(1)} %get-tuple-element.28), channel_id=1, source_target_pairs={{32,0},{64,32},{96,64},{128,96},{160,128},{192,160},{224,192},{256... | collective-permute-start | bytes 294920 | tf_op jit(solution)/shard_map/ppermute | solution.py:24
  296.1 10.4 %copy-start.5 = (f32[10,18,514]{2,1,0:T(8,128)S(1)}, f32[10,18,514]{2,1,0:T(8,128)}, u32[]{:S(2)}) copy-start(f32[10,18,514]{2,1,0:T(8,128)} %get-tuple-element.8) | copy-start | bytes 1110244
  301.2 5.4 %collective-permute-start.10 = (f32[3,10,1,512]{3,2,1,0:T(1,128)S(1)}, f32[3,10,1,512]{3,2,1,0:T(1,128)S(1)}, u32[]{:S(2)}, u32[]{:S(2)}) collective-permute-start(f32[3,10,1,512]{3,2,1,0:T(1,128)S(1)} %get-tuple-element.21), channel_id=1, source_target_pairs={{0,1},{1,2},{2,3},{3,4},{4,5},{5,6},{6,7},{7,8},{8,9},{9,10},{10,1... | collective-permute-start | bytes 184328 | tf_op jit(solution)/shard_map/ppermute | solution.py:23
  303.1 7.1 %collective-permute-start.11 = (f32[3,10,1,512]{3,2,1,0:T(1,128)S(1)}, f32[3,10,1,512]{3,2,1,0:T(1,128)S(1)}, u32[]{:S(2)}, u32[]{:S(2)}) collective-permute-start(f32[3,10,1,512]{3,2,1,0:T(1,128)S(1)} %get-tuple-element.22), channel_id=1, source_target_pairs={{1,0},{2,1},{3,2},{4,3},{5,4},{6,5},{7,6},{8,7},{9,8},{10,9},{11,1... | collective-permute-start | bytes 184328 | tf_op jit(solution)/shard_map/ppermute | solution.py:24
  311.2 0.7 copy-start.12
  313.7 6.0 %collective-permute-start.12 = (f32[1,16,512]{2,1,0:T(8,128)S(1)}, f32[1,16,512]{2,1,0:T(8,128)S(1)}, u32[]{:S(2)}, u32[]{:S(2)}) collective-permute-start(f32[1,16,512]{2,1,0:T(8,128)S(1)} %get-tuple-element.58), channel_id=1, source_target_pairs={{0,32},{32,64},{64,96},{96,128},{128,160},{160,192},{192,224},{224... | collective-permute-start | bytes 98312 | tf_op jit(solution)/shard_map/ppermute | solution.py:23
  316.7 6.4 %collective-permute-start.13 = (f32[1,16,512]{2,1,0:T(8,128)S(1)}, f32[1,16,512]{2,1,0:T(8,128)S(1)}, u32[]{:S(2)}, u32[]{:S(2)}) collective-permute-start(f32[1,16,512]{2,1,0:T(8,128)S(1)} %get-tuple-element.59), channel_id=1, source_target_pairs={{32,0},{64,32},{96,64},{128,96},{160,128},{192,160},{224,192},{256... | collective-permute-start | bytes 98312 | tf_op jit(solution)/shard_map/ppermute | solution.py:24
  323.1 6.0 %collective-permute-start.14 = (f32[10,1,512]{2,1,0:T(1,128)S(1)}, f32[10,1,512]{2,1,0:T(1,128)S(1)}, u32[]{:S(2)}, u32[]{:S(2)}) collective-permute-start(f32[10,1,512]{2,1,0:T(1,128)S(1)} %get-tuple-element.66), channel_id=1, source_target_pairs={{0,1},{1,2},{2,3},{3,4},{4,5},{5,6},{6,7},{7,8},{8,9},{9,10},{10,1... | collective-permute-start | bytes 61448 | tf_op jit(solution)/shard_map/ppermute | solution.py:23
  325.1 6.6 %collective-permute-start.15 = (f32[10,1,512]{2,1,0:T(1,128)S(1)}, f32[10,1,512]{2,1,0:T(1,128)S(1)}, u32[]{:S(2)}, u32[]{:S(2)}) collective-permute-start(f32[10,1,512]{2,1,0:T(1,128)S(1)} %get-tuple-element.67), channel_id=1, source_target_pairs={{1,0},{2,1},{3,2},{4,3},{5,4},{6,5},{7,6},{8,7},{9,8},{10,9},{11,1... | collective-permute-start | bytes 61448 | tf_op jit(solution)/shard_map/ppermute | solution.py:24
  335.9 2.4 copy-start.1
where the time goes:
time: 344 us; the launch traced here: 338 us
  starting transfers between devices  95.5 us (28%)
  local copies, waits for them, and re-layouts  95.3 us (28%)
  waiting for transfers between devices  56 us (16%)
  other arithmetic  42.7 us (12%)
  blocking collectives  41.5 us (12%)
  matrix products  5.88 us (2%)
    scatter x1, local copies, waits for them, and re-layouts, shards(): buffer_momentum = jnp.zeros((n_tile * capacity, 3, 128), jnp.float32).at[...  62.2 us
    ppermute x10, starting transfers between devices, extended(): before = lax.ppermute(last, axis, up)  44 us
    all_gather x1, blocking collectives, shards(): gathered = lax.all_gather(surface_panels, 'tile', axis=0, tiled=True)  41.5 us
    ppermute x10, waiting for transfers between devices, extended(): after = lax.ppermute(initial, axis, down)  31.5 us
    ppermute x10, starting transfers between devices, extended(): after = lax.ppermute(initial, axis, down)  25.4 us
    ppermute x10, waiting for transfers between devices, extended(): before = lax.ppermute(last, axis, up)  24.5 us
    all_to_all x1, starting transfers between devices, shards(): lax.all_to_all(buffer_mass.reshape(n_tile, capacity, 128), 'tile', split_...  9.27 us
    another operation x3, other arithmetic  9.15 us
  transfers between devices with their start and end apart: 23, of which 10 were waited for; matrix products, arithmetic and copies ran while one was open for 33% of the time, Pallas kernels for 0%

commit v1 on v0

v1 whole, which is shorter than its diff:
```python
import jax
import jax.numpy as jnp
from jax import lax
from jax.experimental import pallas as pl
from jax.experimental.pallas import tpu as pltpu
from jax.sharding import PartitionSpec as P

MESH = pl.DeviceIdType.MESH
F32, BF16 = jnp.float32, jnp.bfloat16

relax_factor = 0.8
cell_fraction = 0.1
strain_eps = 0.05
rate_power = -0.4
penalty_factor = 0.5

N_BAND, N_TILE = 16, 32
TX, TY = 4, 8
CZ, CX, CY = 8, 16, 512
OV, NBLK, CAP = 1024, 512, 40
COMPS = 4
GROUP = 4
GROUPS = N_TILE // GROUP
ROWS = GROUP * CAP
SETS = (N_TILE + 2) // 3
RROWS = SETS * 128
TOP = 8


def slot_row(k):
    return 128 * (k // 3) + CAP * (k % 3)


def split2(value):
    high = value.astype(BF16)
    low = (value - high.astype(F32)).astype(BF16)
    return high, low


def iota(shape, dim):
    return lax.broadcasted_iota(jnp.int32, shape, dim)


def ahead_y(f):
    n = f.shape[-1]
    return jnp.where(iota(f.shape, f.ndim - 1) == n - 1, 0.0, pltpu.roll(f, n - 1, f.ndim - 1))


def behind_y(f):
    return jnp.where(iota(f.shape, f.ndim - 1) == 0, 0.0, pltpu.roll(f, 1, f.ndim - 1))


def ahead_x(f, row):
    n = f.shape[0]
    return jnp.where(iota(f.shape, 0) == n - 1, row, pltpu.roll(f, n - 1, 0))


def behind_x(f, row):
    return jnp.where(iota(f.shape, 0) == 0, row, pltpu.roll(f, 1, 0))


def visc_of(squares):
    return jnp.exp(rate_power * jnp.log(strain_eps + squares))


def kernel(
    disp_hbm, mass_hbm, mom_hbm, frac_hbm, order_ref, owner_ref, block_ref,
    kmass_hbm, kmom_hbm, panels_ref, pids_ref, flags_ref,
    regrid_hbm, vel_ref,
    ext, s1, old, frac, kmass, kmom, vol, sel_src, table, send, recv, ids_send, ids_recv,
    sel_dst, xst, xhl, xhr, cst, chl, pans, trac, spd, plane, xm1, xp16, xp17, visc, pres,
    load_sem, out_sem, a2a_send, a2a_recv, ids_ssem, ids_rsem, dh_send, dh_recv,
    py_send, py_recv, px_send, px_recv, sp_send, sp_recv,
):
    b = lax.axis_index("band")
    t = lax.axis_index("tile")
    tx, ty = t // TY, t % TY
    up, down = (b + 1) % N_BAND, (b + N_BAND - 1) % N_BAND
    right, left = (t + 1) % N_TILE, (t + N_TILE - 1) % N_TILE

    def peer(k):
        return ((tx + k // TY) % TX) * TY + (ty + k % TY) % TY

    barrier = pltpu.get_barrier_semaphore()
    partners = [(b, peer(k)) for k in range(1, N_TILE)]
    partners += [(up, t), (down, t), (up, right), (up, left), (down, right), (down, left)]
    for partner in partners:
        pl.semaphore_signal(barrier, inc=1, device_id=partner, device_id_type=MESH)

    loads = [
        pltpu.make_async_copy(disp_hbm, ext.at[:, pl.ds(3, CZ), pl.ds(TOP, CX), :], load_sem.at[0]),
        pltpu.make_async_copy(frac_hbm, frac, load_sem.at[1]),
        pltpu.make_async_copy(mass_hbm, old.at[0], load_sem.at[2]),
        pltpu.make_async_copy(mom_hbm, old.at[pl.ds(1, 3)], load_sem.at[3]),
        pltpu.make_async_copy(kmass_hbm, kmass, load_sem.at[4]),
        pltpu.make_async_copy(kmom_hbm, kmom, load_sem.at[5]),
    ]
    for copy in loads:
        copy.start()

    owner = owner_ref[...]
    column = iota((N_TILE, 1), 0)
    column_dest = ((tx + column // TY) % TX) * TY + (ty + column % TY) % TY
    before = (iota((128, 128), 0) < iota((128, 128), 1)).astype(BF16)
    base = jnp.zeros((N_TILE, 1), F32)
    slots, names = [], []
    for j in range(OV // 128):
        hot = (owner[:, 128 * j : 128 * (j + 1)] == column_dest).astype(F32)
        prefix = base + jnp.dot(hot.astype(BF16), before, preferred_element_type=F32)
        slots.append(jnp.sum(hot * prefix, axis=0, keepdims=True))
        names.append(jnp.sum(hot * column.astype(F32), axis=0, keepdims=True))
        base = base + jnp.sum(hot, axis=1, keepdims=True)
    slot = jnp.concatenate(slots, axis=1)
    name = jnp.concatenate(names, axis=1)
    place = name * CAP + slot
    order = order_ref[...]
    code = (order // 2 + (order % 2) * NBLK + 1).astype(F32)

    block = block_ref[...]
    target = (block % 4) * 128 + block // 4 + 1
    hot = owner == column_dest
    high = jnp.where(hot, target // 16, 0).astype(F32).astype(BF16)
    low = jnp.where(hot, target % 16, 0).astype(F32).astype(BF16)
    lanes = (slot == iota((128, 1), 0).astype(F32)).astype(F32).astype(BF16)
    dims = (((1,), (1,)), ((), ()))
    ids = 16.0 * lax.dot_general(high, lanes, dims, preferred_element_type=F32)
    ids = ids + lax.dot_general(low, lanes, dims, preferred_element_type=F32)
    third = iota((N_TILE, 128), 0) % 3
    ids = jnp.where(
        third == 0, ids, jnp.where(third == 1, pltpu.roll(ids, CAP, 1), pltpu.roll(ids, 2 * CAP, 1))
    )
    for k in range(N_TILE):
        ids_send[k] = ids[k : k + 1, :]
    ids_recv[0] = ids[0:1, :]

    loads[0].wait()
    for c in range(3):
        for k in range(3):
            at = pl.ds(24 * c + 8 * k, 8)
            xst[0, at, :] = ext[c, 3:11, TOP + 13 + k, :]
            xst[1, at, :] = ext[c, 3:11, TOP + k, :]
    for corner in range(4):
        sz, sx = corner // 2, corner % 2
        for c in range(3):
            for i, (dz, dx) in enumerate(((1, 1), (1, 2), (2, 1))):
                z = CZ - dz if sz else dz - 1
                x = CX - dx if sx else dx - 1
                cst[corner, pl.ds(3 * c + i, 1), :] = ext[c, 3 + z, pl.ds(TOP + x, 1), :]
    pans[ty] = panels_ref[...]

    pl.semaphore_wait(barrier, len(partners))

    def remote(src, dst, ssem, rsem, device):
        return pltpu.make_async_remote_copy(
            src_ref=src, dst_ref=dst, send_sem=ssem, recv_sem=rsem, device_id=device, device_id_type=MESH
        )

    disp_copies = [
        remote(xst.at[0], xhl, dh_send.at[0], dh_recv.at[0], (b, right)),
        remote(xst.at[1], xhr, dh_send.at[1], dh_recv.at[1], (b, left)),
        remote(disp_hbm.at[:, pl.ds(CZ - 3, 3)], ext.at[:, pl.ds(0, 3), pl.ds(TOP, CX), :],
               dh_send.at[2], dh_recv.at[2], (up, t)),
        remote(disp_hbm.at[:, pl.ds(0, 3)], ext.at[:, pl.ds(3 + CZ, 3), pl.ds(TOP, CX), :],
               dh_send.at[3], dh_recv.at[3], (down, t)),
    ]
    for corner in range(4):
        sz, sx = corner // 2, corner % 2
        disp_copies.append(
            remote(cst.at[corner], chl.at[corner], dh_send.at[4 + corner], dh_recv.at[4 + corner],
                   (up if sz else down, right if sx else left))
        )
    for copy in disp_copies:
        copy.start()
    panel_y = [
        remote(pans.at[ty], pans.at[ty], py_send.at[i - 1], py_recv.at[i - 1], (b, tx * TY + (ty + i) % TY))
        for i in range(1, TY)
    ]
    for copy in panel_y:
        copy.start()

    ids_copies = [
        remote(ids_send.at[k], ids_recv.at[k], ids_ssem, ids_rsem, (b, peer(k))) for k in range(1, N_TILE)
    ]

    for copy in loads[1:4]:
        copy.wait()

    def fill_table(c):
        share = frac[...]
        values = old[c]
        one = share * values
        high, low = split2(one)
        table[0:NBLK, 0:128] = high
        table[0:NBLK, 128:256] = low
        high, low = split2((1.0 - share) * values)
        table[NBLK : 2 * NBLK, 0:128] = high
        table[NBLK : 2 * NBLK, 128:256] = low

    def rows_copy(c, k):
        return remote(
            send.at[c, pl.ds(CAP * k, CAP), :], recv.at[c, pl.ds(slot_row(k), CAP), :],
            a2a_send.at[c], a2a_recv.at[c], (b, peer(k)),
        )

    def dispatch(c, g):
        both = jnp.dot(sel_src[g], table[...], preferred_element_type=F32)
        rows = both[:, 0:128] + both[:, 128:256]
        send[c, pl.ds(ROWS * g, ROWS), :] = rows
        if g == 0:
            recv[c, 0:CAP, :] = rows[0:CAP]
        for j in range(GROUP):
            k = GROUP * g + j
            if k:
                rows_copy(c, k).start()

    fill_table(0)
    for g in range(GROUPS):
        wanted = (ROWS * g + iota((ROWS, 1), 0)).astype(F32)
        code_of = jnp.sum(jnp.where(place == wanted, code, 0.0), axis=1, keepdims=True)
        hit = code_of.astype(jnp.int32) == iota((ROWS, OV), 1) + 1
        sel_src[g] = jnp.where(hit, 1.0, 0.0).astype(BF16)
        dispatch(0, g)
        if g == 0:
            for copy in ids_copies:
                copy.start()

    for i, copy in enumerate(panel_y):
        copy.wait()

    panel_x = [
        remote(pans.at[pl.ds(0, TY)], pans.at[pl.ds(TY * i, TY)], px_send.at[i - 1], px_recv.at[i - 1],
               (b, ((tx + i) % TX) * TY + ty))
        for i in range(1, TX)
    ]
    for copy in panel_x:
        copy.start()

    def later(c, carry):
        fill_table(c)
        for g in range(GROUPS):
            dispatch(c, g)
        return carry

    lax.fori_loop(1, COMPS, later, 0)

    for copy in disp_copies:
        copy.wait()
    at_left, at_right = t == 0, t == N_TILE - 1
    at_bottom, at_top = b == 0, b == N_BAND - 1
    nothing = jnp.zeros((8, CY), F32)
    for c in range(3):
        for k in range(3):
            at = pl.ds(24 * c + 8 * k, 8)
            ext[c, 3:11, TOP - 3 + k, :] = jnp.where(at_left, nothing, xhl[at, :])
            ext[c, 3:11, TOP + CX + k, :] = jnp.where(at_right, nothing, xhr[at, :])

    @pl.when(at_bottom)
    def _():
        ext[:, 0:3, TOP : TOP + CX, :] = jnp.zeros((3, 3, CX, CY), F32)

    @pl.when(at_top)
    def _():
        ext[:, 3 + CZ : 6 + CZ, TOP : TOP + CX, :] = jnp.zeros((3, 3, CX, CY), F32)

    for corner in range(4):
        sz, sx = corner // 2, corner % 2
        outside = (at_bottom if sz else at_top) | (at_left if sx else at_right)
        for c in range(3):
            for i, (dz, dx) in enumerate(((1, 1), (1, 2), (2, 1))):
                z = -dz if sz else CZ - 1 + dz
                x = -dx if sx else CX - 1 + dx
                line = chl[corner, pl.ds(3 * c + i, 1), :]
                ext[c, 3 + z, pl.ds(TOP + x, 1), :] = jnp.where(outside, jnp.zeros_like(line), line)

    row = iota((32, CY), 0) - TOP
    keep_x = ((row >= 0) | jnp.logical_not(at_left)) & ((row < CX) | jnp.logical_not(at_right))

    def sweep(src, dst, c, zi):
        here = src[c, zi]
        near = src[c, zi + 1] + src[c, zi - 1]
        near = near + pltpu.roll(here, 1, 0) + pltpu.roll(here, 31, 0)
        near = near + ahead_y(here) + behind_y(here)
        new = here + relax_factor * (near / 6.0 - here)
        z = zi - 3
        inside = ((z >= 0) | jnp.logical_not(at_bottom)) & ((z < CZ) | jnp.logical_not(at_top))
        dst[c, zi] = jnp.where(keep_x & inside, new, 0.0)

    def first(zi, carry):
        for c in range(3):
            sweep(ext, s1, c, zi)
        return carry

    def second(zi, carry):
        for c in range(3):
            sweep(s1, ext, c, zi)
        return carry

    lax.fori_loop(1, 13, first, 0)
    lax.fori_loop(2, 12, second, 0)
    regrid_out = pltpu.make_async_copy(
        ext.at[:, pl.ds(3, CZ), pl.ds(TOP, CX), :], regrid_hbm, out_sem.at[0]
    )
    regrid_out.start()

    def volumes(z, carry):
        zi = z + 3
        own = pl.ds(TOP, CX)
        stretch = ext[0, zi + 1, own, :] - ext[0, zi - 1, own, :]
        across = ext[1, zi]
        across = pltpu.roll(across, 31, 0) - pltpu.roll(across, 1, 0)
        along = ext[2, zi, own, :]
        stretch = stretch + across[TOP : TOP + CX] + (ahead_y(along) - behind_y(along))
        vol[z] = 1.0 + cell_fraction * (0.5 * stretch)
        return carry

    lax.fori_loop(0, CZ, volumes, 0)

    for copy in panel_x:
        copy.wait()
    source = iota((N_TILE * 4, CX), 0)
    member = source // 4
    panel = ((tx + TX - member // TY) % TX) * (TY * 4) + (member % TY) * 4 + source % 4
    for yb in range(CY // 128):
        chosen = (panel == pids_ref[yb : yb + 1, :]) & (flags_ref[yb : yb + 1, :] != 0)
        chosen = jnp.where(chosen, 1.0, 0.0)
        for c in range(3):
            faces = pans[:, c].reshape(N_TILE * 4, 128)
            high, low = split2(faces)
            tn = (((0,), (0,)), ((), ()))
            weight = chosen.astype(BF16)
            got = lax.dot_general(weight, high, tn, preferred_element_type=F32)
            got = got + lax.dot_general(weight, low, tn, preferred_element_type=F32)
            trac[c, :, 128 * yb : 128 * (yb + 1)] = got

    bulk = (N_TILE - 1) * CAP
    pltpu.make_async_copy(ids_recv.at[pl.ds(1, N_TILE - 1)], ids_recv.at[pl.ds(1, N_TILE - 1)], ids_rsem).wait()
    number = iota((NBLK, 128), 0).astype(F32) + 1.0
    for s in range(SETS):
        line = ids_recv[3 * s]
        for k in range(3 * s + 1, min(3 * s + 3, N_TILE)):
            line = line + ids_recv[k]
        sel_dst[:, 128 * s : 128 * (s + 1)] = jnp.where(number == line, 1.0, 0.0).astype(BF16)
    for s in range(SETS):
        used = CAP * min(3, N_TILE - 3 * s)
        for c in range(COMPS):
            recv[c, 128 * s + used : 128 * (s + 1), :] = jnp.zeros((128 - used, 128), F32)

    def incoming(c):
        pltpu.make_async_copy(recv.at[c, pl.ds(0, bulk)], recv.at[c, pl.ds(0, bulk)], a2a_recv.at[c]).wait()
        high, low = split2(recv[c])
        both = jnp.dot(sel_dst[...], jnp.concatenate([high, low], axis=1), preferred_element_type=F32)
        total = both[:, 0:128] + both[:, 128:256]
        return [total[128 * yb : 128 * (yb + 1)].reshape(CZ, CX, 128) for yb in range(CY // 128)]

    for copy in loads[4:]:
        copy.wait()
    for yb, more in enumerate(incoming(0)):
        at = pl.ds(128 * yb, 128)
        kmass[:, :, at] = kmass[:, :, at] + more

    spd_copies = []
    for c in range(3):
        for yb, more in enumerate(incoming(c + 1)):
            at = pl.ds(128 * yb, 128)
            spd[c, 1 : 1 + CZ, :, at] = (kmom[c, :, :, at] + more) / kmass[:, :, at]
        plane[c, 0:8, :] = spd[c, 1 : 1 + CZ, 0, :]
        plane[c, 8:16, :] = spd[c, 1 : 1 + CZ, 1, :]
        plane[c, 16:24, :] = spd[c, 1 : 1 + CZ, CX - 1, :]
        first_x, second_x, last_x = (plane.at[c, pl.ds(8 * i, 8), :] for i in range(3))
        moves = [
            (spd.at[c, CZ], spd.at[c, 0], (up, t)),
            (spd.at[c, pl.ds(1, 2)], spd.at[c, pl.ds(1 + CZ, 2)], (down, t)),
            (first_x, xp16.at[c, pl.ds(8, 8), :], (b, left)),
            (second_x, xp17.at[c], (b, left)),
            (last_x, xm1.at[c, pl.ds(0, 8), :], (b, right)),
            (last_x, xm1.at[c, pl.ds(8, 8), :], (down, right)),
            (first_x, xp16.at[c, pl.ds(0, 8), :], (up, left)),
            (first_x, xp16.at[c, pl.ds(16, 8), :], (down, left)),
        ]
        for i, (src, dst, device) in enumerate(moves):
            copy = remote(src, dst, sp_send.at[c, i], sp_recv.at[c, i], device)
            copy.start()
            spd_copies.append(copy)
    for copy in spd_copies:
        copy.wait()

    @pl.when(at_bottom)
    def _():
        for c in range(3):
            spd[c, 0] = jnp.zeros((CX, CY), F32)
            xp16[c, 0:8, :] = nothing

    @pl.when(at_top)
    def _():
        for c in range(3):
            spd[c, 1 + CZ : 3 + CZ] = jnp.zeros((2, CX, CY), F32)
            xm1[c, 8:16, :] = nothing
            xp16[c, 16:24, :] = nothing

    @pl.when(at_left)
    def _():
        for c in range(3):
            xm1[c] = jnp.zeros((16, CY), F32)

    @pl.when(at_right)
    def _():
        for c in range(3):
            xp16[c] = jnp.zeros((24, CY), F32)
            xp17[c] = nothing

    def squared(here, *others):
        total = jnp.zeros_like(here)
        for other in others:
            change = other - here
            total = total + change * change
        return total

    squares_m = jnp.zeros((CZ, CY), F32)
    squares_p = jnp.zeros((CZ, CY), F32)
    for c in range(3):
        whole = xm1[c]
        here = whole[0:8]
        above = pltpu.roll(whole, 15, 0)[0:8]
        squares_m = squares_m + squared(here, above, plane[c, 0:8, :], ahead_y(here))
        whole = xp16[c]
        here = whole[8:16]
        above = pltpu.roll(whole, 23, 0)[8:16]
        squares_p = squares_p + squared(here, above, xp17[c], ahead_y(here))
    visc_m = jnp.where(at_left, 0.0, visc_of(squares_m))
    visc_p = jnp.where(at_right, 0.0, visc_of(squares_p))
    plane[0, 0:8, :] = visc_m
    plane[0, 8:16, :] = visc_p
    here = xp16[0]
    div = here[8:16] - pltpu.roll(here, 1, 0)[8:16]
    div = div + (xp16[1, 8:16, :] - plane[1, 16:24, :])
    here = xp16[2, 8:16, :]
    div = div + (here - behind_y(here))
    plane[0, 16:24, :] = jnp.where(at_right, 0.0, -penalty_factor * div)

    def viscosity(i, carry):
        squares = jnp.zeros((CX, CY), F32)
        for c in range(3):
            here = spd[c, i]
            edge = xp16[c, pl.ds(i + 7, 1), :]
            squares = squares + squared(here, spd[c, i + 1], ahead_x(here, edge), ahead_y(here))
        z = i - 1
        inside = ((z >= 0) | jnp.logical_not(at_bottom)) & ((z < CZ) | jnp.logical_not(at_top))
        visc[i] = jnp.where(inside, visc_of(squares), 0.0)
        return carry

    lax.fori_loop(0, CZ + 2, viscosity, 0)

    def pressure(z, carry):
        here = spd[0, z + 1]
        div = here - spd[0, z]
        here = spd[1, z + 1]
        div = div + (here - behind_x(here, xm1[1, pl.ds(z, 1), :]))
        here = spd[2, z + 1]
        div = div + (here - behind_y(here))
        inside = (z < CZ) | jnp.logical_not(at_top)
        pres[z] = jnp.where(inside, -penalty_factor * div, 0.0)
        return carry

    lax.fori_loop(0, CZ + 1, pressure, 0)

    def update(z, carry):
        v = visc[z + 1]
        line = pl.ds(z, 1)
        v_next = (visc[z + 2], ahead_x(v, plane[0, pl.ds(z + 8, 1), :]), ahead_y(v))
        v_prev = (visc[z], behind_x(v, plane[0, line, :]), behind_y(v))
        forward = [0.5 * (v + other) for other in v_next]
        backward = [0.5 * (v + other) for other in v_prev]
        density = kmass[z] / vol[z]
        bottom = forward[0] + backward[0] + forward[1] + backward[1] + forward[2] + backward[2] + density
        p = pres[z]
        p_next = (pres[z + 1], ahead_x(p, plane[0, pl.ds(z + 16, 1), :]), ahead_y(p))
        for c in range(3):
            here = spd[c, z + 1]
            top = forward[0] * spd[c, z + 2] + backward[0] * spd[c, z]
            top = top + forward[1] * ahead_x(here, xp16[c, pl.ds(z + 8, 1), :])
            top = top + backward[1] * behind_x(here, xm1[c, line, :])
            top = top + forward[2] * ahead_y(here) + backward[2] * behind_y(here)
            top = top - (p_next[c] - p) + trac[c] + density * here
            vel_ref[c, z] = top / bottom
        return carry

    lax.fori_loop(0, CZ, update, 0)

    for c in range(COMPS):
        pltpu.make_async_copy(send.at[c, pl.ds(0, bulk)], send.at[c, pl.ds(0, bulk)], a2a_send.at[c]).wait()
    pltpu.make_async_copy(ids_send.at[pl.ds(1, N_TILE - 1)], ids_send.at[pl.ds(1, N_TILE - 1)], ids_ssem).wait()
    regrid_out.wait()


def shards(
    displacement, old_mass, old_momentum, intersection_fraction, entry_order, target_owner,
    target_block, kept_mass, kept_momentum, surface_panels, panel_ids, contact_flags,
):
    grid = jax.ShapeDtypeStruct((3, CZ, CX, CY), F32)
    hbm, vmem = pl.BlockSpec(memory_space=pl.ANY), pl.BlockSpec(memory_space=pltpu.VMEM)
    dma = pltpu.SemaphoreType.DMA
    return pl.pallas_call(
        kernel,
        out_shape=(grid, grid),
        in_specs=[hbm, hbm, hbm, hbm, vmem, vmem, vmem, hbm, hbm, vmem, vmem, vmem],
        out_specs=(hbm, vmem),
        scratch_shapes=[
            pltpu.VMEM((3, CZ + 6, 32, CY), F32),
            pltpu.VMEM((3, CZ + 6, 32, CY), F32),
            pltpu.VMEM((COMPS, NBLK, 128), F32),
            pltpu.VMEM((NBLK, 128), F32),
            pltpu.VMEM((CZ, CX, CY), F32),
            pltpu.VMEM((3, CZ, CX, CY), F32),
            pltpu.VMEM((CZ, CX, CY), F32),
            pltpu.VMEM((GROUPS, ROWS, OV), BF16),
            pltpu.VMEM((2 * NBLK, 256), BF16),
            pltpu.VMEM((COMPS, N_TILE * CAP, 128), F32),
            pltpu.VMEM((COMPS, RROWS, 128), F32),
            pltpu.VMEM((N_TILE, 1, 128), F32),
            pltpu.VMEM((N_TILE, 1, 128), F32),
            pltpu.VMEM((NBLK, RROWS), BF16),
            pltpu.VMEM((2, 72, CY), F32),
            pltpu.VMEM((72, CY), F32),
            pltpu.VMEM((72, CY), F32),
            pltpu.VMEM((4, 16, CY), F32),
            pltpu.VMEM((4, 16, CY), F32),
            pltpu.VMEM((N_TILE, 3, 4, 128), F32),
            pltpu.VMEM((3, CX, CY), F32),
            pltpu.VMEM((3, CZ + 3, CX, CY), F32),
            pltpu.VMEM((3, 24, CY), F32),
            pltpu.VMEM((3, 16, CY), F32),
            pltpu.VMEM((3, 24, CY), F32),
            pltpu.VMEM((3, 8, CY), F32),
            pltpu.VMEM((CZ + 2, CX, CY), F32),
            pltpu.VMEM((CZ + 1, CX, CY), F32),
            dma((6,)),
            dma((1,)),
            dma((COMPS,)),
            dma((COMPS,)),
            dma,
            dma,
            dma((8,)),
            dma((8,)),
            dma((TY - 1,)),
            dma((TY - 1,)),
            dma((TX - 1,)),
            dma((TX - 1,)),
            dma((3, 8)),
            dma((3, 8)),
        ],
        compiler_params=pltpu.CompilerParams(
            collective_id=0, has_side_effects=True, vmem_limit_bytes=48 * 2**20
        ),
    )(
        displacement,
        old_mass,
        old_momentum.transpose(1, 0, 2),
        intersection_fraction,
        entry_order,
        target_owner.reshape(1, OV),
        target_block.reshape(1, OV),
        kept_mass,
        kept_momentum,
        surface_panels.transpose(1, 0, 2),
        panel_ids[0].T,
        contact_flags[0].T,
    )


def solution(mesh):
    return jax.shard_map(
        shards,
        mesh=mesh,
        in_specs=(
            P(None, "band", "tile", None),
            P(("band", "tile"), None),
            P(("band", "tile"), None, None),
            P(("band", "tile"), None),
            P(("band", "tile"), None),
            P(("band", "tile"), None),
            P(("band", "tile")),
            P("band", "tile", None),
            P(None, "band", "tile", None),
            P(("band", "tile"), None, None),
            P("band", "tile", None),
            P("band", "tile", None),
        ),
        out_specs=(P(None, "band", "tile", None), P(None, "band", "tile", None)),
        check_vma=False,
    )
```

time: 344 us -> 101 us (0.29)
  the two profiles are of different devices: /device:TPU:249 before, /device:TPU:193 now
where the time goes in v1:
time: 101 us
  Pallas kernels  88.6 us (88%)
  local copies, waits for them, and re-layouts  11.4 us (11%)
    pallas_call x1, Pallas kernels, shards(): pl.pallas_call(kernel, out_shape=(grid, grid), in_specs=[hbm, hbm, hbm, h...  88.6 us
    unnamed x26, local copies, waits for them, and re-layouts  11.4 us

profile of v1, /device:TPU:193, one launch (start us, length us, event | category | flops | bytes accessed | tf_op | source)
XLA Modules:
  0.0 100.7 jit_solution(5841658818856875061)
XLA Ops:
  0.6 0.0 copy-start.6
  0.6 0.0 copy-start.7
  0.7 0.7 copy-done.6
  1.3 0.0 copy-done.7
  1.3 0.0 copy-start
  1.3 1.1 %copy-done = f32[3,8,16,512]{3,2,1,0:T(8,128)S(1)} copy-done((f32[3,8,16,512]{3,2,1,0:T(8,128)S(1)}, f32[3,8,16,512]{3,2,1,0:T(8,128)}, u32[]{:S(2)}) %copy-start) | copy-done | bytes 786456
  2.5 0.0 copy-start.1
  2.5 1.1 %copy-done.1 = f32[512,3,128]{2,0,1:T(8,128)S(1)} copy-done((f32[512,3,128]{2,0,1:T(8,128)S(1)}, f32[512,3,128]{2,0,1:T(8,128)}, u32[]{:S(2)}) %copy-start.1) | copy-done | bytes 786456
  3.6 0.0 copy-start.2
  3.6 1.1 %copy-done.2 = f32[3,8,16,512]{3,2,1,0:T(8,128)S(1)} copy-done((f32[3,8,16,512]{3,2,1,0:T(8,128)S(1)}, f32[3,8,16,512]{3,2,1,0:T(8,128)}, u32[]{:S(2)}) %copy-start.2) | copy-done | bytes 786456
  4.7 0.0 copy-start.3
  4.7 0.9 copy-done.3
  5.7 0.0 copy-start.4
  5.7 0.9 copy-done.4
  6.6 0.0 copy-start.5
  6.6 0.9 copy-done.5
  7.6 0.0 copy-start.8
  7.6 0.7 copy-done.8
  8.3 0.0 copy-start.9
  8.3 0.7 copy-done.9
  9.0 0.0 copy-start.10
  9.0 0.7 copy-done.10
  9.6 0.0 copy-start.11
  9.7 0.7 copy-done.11
  10.3 88.6 %shard_map.131 = (f32[3,8,16,512]{3,2,1,0:T(8,128)S(1)}, f32[3,8,16,512]{3,2,1,0:T(8,128)S(1)}) custom-call(f32[3,8,16,512]{3,2,1,0:T(8,128)S(1)} %copy-done, f32[512,128]{1,0:T(8,128)S(1)} %copy-done.3, f32[3,512,128]{2,1,0:T(8,128)S(1)} %bitcast.10, f32[512,128]{1,0:T(8,128)S(1)} %copy-done.4, s32[1,1024]{1,0:T(1,128)S(1)} %copy-done.7, ...), custom_call_target="tpu_custom_call" | custom-call | tf_op jit(solution)/shard_map/pallas_call | solution.py:502
  98.9 0.9 copy.16
  99.8 0.9 copy.17
Async XLA Ops:
  0.6 0.7 copy-start.6
  0.6 0.7 copy-start.7
  1.3 1.1 %copy-start = (f32[3,8,16,512]{3,2,1,0:T(8,128)S(1)}, f32[3,8,16,512]{3,2,1,0:T(8,128)}, u32[]{:S(2)}) copy-start(f32[3,8,16,512]{3,2,1,0:T(8,128)} %disp_hbm.1) | copy-start | bytes 2359300
  2.5 1.1 %copy-start.1 = (f32[512,3,128]{2,0,1:T(8,128)S(1)}, f32[512,3,128]{2,0,1:T(8,128)}, u32[]{:S(2)}) copy-start(f32[512,3,128]{2,0,1:T(8,128)} %param.14) | copy-start | bytes 2359300
  3.6 1.1 %copy-start.2 = (f32[3,8,16,512]{3,2,1,0:T(8,128)S(1)}, f32[3,8,16,512]{3,2,1,0:T(8,128)}, u32[]{:S(2)}) copy-start(f32[3,8,16,512]{3,2,1,0:T(8,128)} %kmom_hbm.1) | copy-start | bytes 2359300
  4.7 0.9 copy-start.3
  5.7 0.9 copy-start.4
  6.6 0.9 copy-start.5
  7.6 0.7 copy-start.8
  8.3 0.7 copy-start.9
  9.0 0.7 copy-start.10
  9.6 0.7 copy-start.11

commit v2 on v1

--- a/solution.py
+++ b/solution.py
@@ -25,6 +25,9 @@
 SETS = (N_TILE + 2) // 3
 RROWS = SETS * 128
 TOP = 8
+PLANES = ((0, 1), (0, 2), (1, 1), (1, 2), (1, 3), (2, 1), (2, 2))
+LINES = ((0, 1, 1), (0, 1, 2), (0, 2, 1), (1, 1, 1), (1, 1, 2), (1, 2, 1), (2, 1, 1))
+PARTS = ((0, 4), (4, 8), (8, SETS))
 
 
 def slot_row(k):
@@ -64,12 +67,13 @@
 
 
 def kernel(
-    disp_hbm, mass_hbm, mom_hbm, frac_hbm, order_ref, owner_ref, block_ref,
-    kmass_hbm, kmom_hbm, panels_ref, pids_ref, flags_ref,
-    regrid_hbm, vel_ref,
+    disp_hbm, mass_hbm, mom_hbm, frac_hbm, order_hbm, owner_hbm, block_hbm,
+    kmass_hbm, kmom_hbm, panels_hbm, pids_hbm, flags_hbm,
+    regrid_ref, vel_ref,
+    order_ref, owner_ref, block_ref, panels_ref, pids_ref, flags_ref,
     ext, s1, old, frac, kmass, kmom, vol, sel_src, table, send, recv, ids_send, ids_recv,
-    sel_dst, xst, xhl, xhr, cst, chl, pans, trac, spd, plane, xm1, xp16, xp17, visc, pres,
-    load_sem, out_sem, a2a_send, a2a_recv, ids_ssem, ids_rsem, dh_send, dh_recv,
+    sel_dst, xst, xhl, xhr, cst, chl, pans, trac, spd, plane, xm1, xp16, qst, xq, crs, crn, side, visc, pres,
+    small_sem, load_sem, out_sem, a2a_send, a2a_recv, ids_ssem, ids_rsem, dh_send, dh_recv,
     py_send, py_recv, px_send, px_recv, sp_send, sp_recv,
 ):
     b = lax.axis_index("band")
@@ -87,6 +91,9 @@
     for partner in partners:
         pl.semaphore_signal(barrier, inc=1, device_id=partner, device_id_type=MESH)
 
+    small = [(owner_hbm, owner_ref), (order_hbm, order_ref), (block_hbm, block_ref),
+             (panels_hbm, panels_ref), (pids_hbm, pids_ref), (flags_hbm, flags_ref)]
+    small = [pltpu.make_async_copy(src, dst, small_sem.at[i]) for i, (src, dst) in enumerate(small)]
     loads = [
         pltpu.make_async_copy(disp_hbm, ext.at[:, pl.ds(3, CZ), pl.ds(TOP, CX), :], load_sem.at[0]),
         pltpu.make_async_copy(frac_hbm, frac, load_sem.at[1]),
@@ -95,57 +102,23 @@
         pltpu.make_async_copy(kmass_hbm, kmass, load_sem.at[4]),
         pltpu.make_async_copy(kmom_hbm, kmom, load_sem.at[5]),
     ]
-    for copy in loads:
+    loads[0].start()
+    for copy in small + loads[1:]:
         copy.start()
 
-    owner = owner_ref[...]
-    column = iota((N_TILE, 1), 0)
-    column_dest = ((tx + column // TY) % TX) * TY + (ty + column % TY) % TY
-    before = (iota((128, 128), 0) < iota((128, 128), 1)).astype(BF16)
-    base = jnp.zeros((N_TILE, 1), F32)
-    slots, names = [], []
-    for j in range(OV // 128):
-        hot = (owner[:, 128 * j : 128 * (j + 1)] == column_dest).astype(F32)
-        prefix = base + jnp.dot(hot.astype(BF16), before, preferred_element_type=F32)
-        slots.append(jnp.sum(hot * prefix, axis=0, keepdims=True))
-        names.append(jnp.sum(hot * column.astype(F32), axis=0, keepdims=True))
-        base = base + jnp.sum(hot, axis=1, keepdims=True)
-    slot = jnp.concatenate(slots, axis=1)
-    name = jnp.concatenate(names, axis=1)
-    place = name * CAP + slot
-    order = order_ref[...]
-    code = (order // 2 + (order % 2) * NBLK + 1).astype(F32)
-
-    block = block_ref[...]
-    target = (block % 4) * 128 + block // 4 + 1
-    hot = owner == column_dest
-    high = jnp.where(hot, target // 16, 0).astype(F32).astype(BF16)
-    low = jnp.where(hot, target % 16, 0).astype(F32).astype(BF16)
-    lanes = (slot == iota((128, 1), 0).astype(F32)).astype(F32).astype(BF16)
-    dims = (((1,), (1,)), ((), ()))
-    ids = 16.0 * lax.dot_general(high, lanes, dims, preferred_element_type=F32)
-    ids = ids + lax.dot_general(low, lanes, dims, preferred_element_type=F32)
-    third = iota((N_TILE, 128), 0) % 3
-    ids = jnp.where(
-        third == 0, ids, jnp.where(third == 1, pltpu.roll(ids, CAP, 1), pltpu.roll(ids, 2 * CAP, 1))
-    )
-    for k in range(N_TILE):
-        ids_send[k] = ids[k : k + 1, :]
-    ids_recv[0] = ids[0:1, :]
-
     loads[0].wait()
-    for c in range(3):
-        for k in range(3):
-            at = pl.ds(24 * c + 8 * k, 8)
-            xst[0, at, :] = ext[c, 3:11, TOP + 13 + k, :]
-            xst[1, at, :] = ext[c, 3:11, TOP + k, :]
+    for i, (c, d) in enumerate(PLANES):
+        at = pl.ds(8 * i, 8)
+        xst[0, at, :] = ext[c, 3:11, TOP + CX - d, :]
+        xst[1, at, :] = ext[c, 3:11, TOP + d - 1, :]
     for corner in range(4):
         sz, sx = corner // 2, corner % 2
-        for c in range(3):
-            for i, (dz, dx) in enumerate(((1, 1), (1, 2), (2, 1))):
-                z = CZ - dz if sz else dz - 1
-                x = CX - dx if sx else dx - 1
-                cst[corner, pl.ds(3 * c + i, 1), :] = ext[c, 3 + z, pl.ds(TOP + x, 1), :]
+        for i, (c, dz, dx) in enumerate(LINES):
+            z = CZ - dz if sz else dz - 1
+            x = CX - dx if sx else dx - 1
+            cst[corner, i] = ext[c, 3 + z, pl.ds(TOP + x, 1), :]
+    for copy in small:
+        copy.wait()
     pans[ty] = panels_ref[...]
 
     pl.semaphore_wait(barrier, len(partners))
@@ -178,9 +151,47 @@
     for copy in panel_y:
         copy.start()
 
+    owner = owner_ref[...]
+    column = iota((N_TILE, 1), 0)
+    column_dest = ((tx + column // TY) % TX) * TY + (ty + column % TY) % TY
+    before = (iota((128, 128), 0) < iota((128, 128), 1)).astype(BF16)
+    base = jnp.zeros((N_TILE, 1), F32)
+    slots, names = [], []
+    for j in range(OV // 128):
+        hot = (owner[:, 128 * j : 128 * (j + 1)] == column_dest).astype(F32)
+        prefix = base + jnp.dot(hot.astype(BF16), before, preferred_element_type=F32)
+        slots.append(jnp.sum(hot * prefix, axis=0, keepdims=True))
+        names.append(jnp.sum(hot * column.astype(F32), axis=0, keepdims=True))
+        base = base + jnp.sum(hot, axis=1, keepdims=True)
+    slot = jnp.concatenate(slots, axis=1)
+    name = jnp.concatenate(names, axis=1)
+    place = name * CAP + slot
+    order = order_ref[...]
+    code = (order // 2 + (order % 2) * NBLK + 1).astype(F32)
+
+    block = block_ref[...]
+    target = (block % 4) * 128 + block // 4 + 1
+    hot = owner == column_dest
+    high = jnp.where(hot, target // 16, 0).astype(F32).astype(BF16)
+    low = jnp.where(hot, target % 16, 0).astype(F32).astype(BF16)
+    lanes = (slot == iota((128, 1), 0).astype(F32)).astype(F32).astype(BF16)
+    dims = (((1,), (1,)), ((), ()))
+    ids = 16.0 * lax.dot_general(high, lanes, dims, preferred_element_type=F32)
+    ids = ids + lax.dot_general(low, lanes, dims, preferred_element_type=F32)
+    third = iota((N_TILE, 128), 0) % 3
+    ids = jnp.where(
+        third == 0, ids, jnp.where(third == 1, pltpu.roll(ids, CAP, 1), pltpu.roll(ids, 2 * CAP, 1))
+    )
+    for k in range(N_TILE):
+        ids_send[k] = ids[k : k + 1, :]
+    ids_recv[0] = ids[0:1, :]
+
     ids_copies = [
         remote(ids_send.at[k], ids_recv.at[k], ids_ssem, ids_rsem, (b, peer(k))) for k in range(1, N_TILE)
     ]
+
+    for copy in ids_copies:
+        copy.start()
 
     for copy in loads[1:4]:
         copy.wait()
@@ -199,7 +210,7 @@
     def rows_copy(c, k):
         return remote(
             send.at[c, pl.ds(CAP * k, CAP), :], recv.at[c, pl.ds(slot_row(k), CAP), :],
-            a2a_send.at[c], a2a_recv.at[c], (b, peer(k)),
+            a2a_send.at[c], a2a_recv.at[c + (c // 3) * (k // 12)], (b, peer(k)),
         )
 
     def dispatch(c, g):
@@ -220,9 +231,6 @@
         hit = code_of.astype(jnp.int32) == iota((ROWS, OV), 1) + 1
         sel_src[g] = jnp.where(hit, 1.0, 0.0).astype(BF16)
         dispatch(0, g)
-        if g == 0:
-            for copy in ids_copies:
-                copy.start()
 
     for i, copy in enumerate(panel_y):
         copy.wait()
@@ -248,11 +256,10 @@
     at_left, at_right = t == 0, t == N_TILE - 1
     at_bottom, at_top = b == 0, b == N_BAND - 1
     nothing = jnp.zeros((8, CY), F32)
-    for c in range(3):
-        for k in range(3):
-            at = pl.ds(24 * c + 8 * k, 8)
-            ext[c, 3:11, TOP - 3 + k, :] = jnp.where(at_left, nothing, xhl[at, :])
-            ext[c, 3:11, TOP + CX + k, :] = jnp.where(at_right, nothing, xhr[at, :])
+    for i, (c, d) in enumerate(PLANES):
+        at = pl.ds(8 * i, 8)
+        ext[c, 3:11, TOP - d, :] = jnp.where(at_left, nothing, xhl[at, :])
+        ext[c, 3:11, TOP + CX - 1 + d, :] = jnp.where(at_right, nothing, xhr[at, :])
 
     @pl.when(at_bottom)
     def _():
@@ -265,12 +272,11 @@
     for corner in range(4):
         sz, sx = corner // 2, corner % 2
         outside = (at_bottom if sz else at_top) | (at_left if sx else at_right)
-        for c in range(3):
-            for i, (dz, dx) in enumerate(((1, 1), (1, 2), (2, 1))):
-                z = -dz if sz else CZ - 1 + dz
-                x = -dx if sx else CX - 1 + dx
-                line = chl[corner, pl.ds(3 * c + i, 1), :]
-                ext[c, 3 + z, pl.ds(TOP + x, 1), :] = jnp.where(outside, jnp.zeros_like(line), line)
+        for i, (c, dz, dx) in enumerate(LINES):
+            z = -dz if sz else CZ - 1 + dz
+            x = -dx if sx else CX - 1 + dx
+            line = chl[corner, i]
+            ext[c, 3 + z, pl.ds(TOP + x, 1), :] = jnp.where(outside, jnp.zeros_like(line), line)
 
     row = iota((32, CY), 0) - TOP
     keep_x = ((row >= 0) | jnp.logical_not(at_left)) & ((row < CX) | jnp.logical_not(at_right))
@@ -298,7 +304,7 @@
     lax.fori_loop(1, 13, first, 0)
     lax.fori_loop(2, 12, second, 0)
     regrid_out = pltpu.make_async_copy(
-        ext.at[:, pl.ds(3, CZ), pl.ds(TOP, CX), :], regrid_hbm, out_sem.at[0]
+        ext.at[:, pl.ds(3, CZ), pl.ds(TOP, CX), :], regrid_ref, out_sem.at[0]
     )
     regrid_out.start()
 
@@ -345,11 +351,19 @@
         for c in range(COMPS):
             recv[c, 128 * s + used : 128 * (s + 1), :] = jnp.zeros((128 - used, 128), F32)
 
+    def arrived(c, first, last, sem):
+        rows = CAP * (min(3 * last, N_TILE) - max(3 * first, 1))
+        pltpu.make_async_copy(recv.at[c, pl.ds(0, rows)], recv.at[c, pl.ds(0, rows)], sem).wait()
+        at = pl.ds(128 * first, 128 * (last - first))
+        high, low = split2(recv[c, at, :])
+        both = jnp.dot(sel_dst[:, at], jnp.concatenate([high, low], axis=1), preferred_element_type=F32)
+        return both[:, 0:128] + both[:, 128:256]
+
     def incoming(c):
-        pltpu.make_async_copy(recv.at[c, pl.ds(0, bulk)], recv.at[c, pl.ds(0, bulk)], a2a_recv.at[c]).wait()
-        high, low = split2(recv[c])
-        both = jnp.dot(sel_dst[...], jnp.concatenate([high, low], axis=1), preferred_element_type=F32)
-        total = both[:, 0:128] + both[:, 128:256]
+        if c < 3:
+            total = arrived(c, 0, SETS, a2a_recv.at[c])
+        else:
+            total = sum(arrived(c, *part, a2a_recv.at[c + i]) for i, part in enumerate(PARTS))
         return [total[128 * yb : 128 * (yb + 1)].reshape(CZ, CX, 128) for yb in range(CY // 128)]
 
     for copy in loads[4:]:
@@ -359,54 +373,40 @@
         kmass[:, :, at] = kmass[:, :, at] + more
 
     spd_copies = []
+
+    def send_speed(moves):
+        for src, dst, device in moves:
+            i = len(spd_copies)
+            spd_copies.append(remote(src, dst, sp_send.at[i], sp_recv.at[i], device))
+            spd_copies[-1].start()
+
+    across = jnp.zeros((CZ, CY), F32)
     for c in range(3):
         for yb, more in enumerate(incoming(c + 1)):
             at = pl.ds(128 * yb, 128)
             spd[c, 1 : 1 + CZ, :, at] = (kmom[c, :, :, at] + more) / kmass[:, :, at]
-        plane[c, 0:8, :] = spd[c, 1 : 1 + CZ, 0, :]
-        plane[c, 8:16, :] = spd[c, 1 : 1 + CZ, 1, :]
-        plane[c, 16:24, :] = spd[c, 1 : 1 + CZ, CX - 1, :]
-        first_x, second_x, last_x = (plane.at[c, pl.ds(8 * i, 8), :] for i in range(3))
-        moves = [
+        first_x = spd[c, 1 : 1 + CZ, 0, :]
+        last_x = spd[c, 1 : 1 + CZ, CX - 1, :]
+        plane[c, 0:8, :] = first_x
+        plane[c, 8:16, :] = last_x
+        send_speed((
+            (plane.at[c, pl.ds(0, 8), :], xp16.at[c, pl.ds(8, 8), :], (b, left)),
+            (plane.at[c, pl.ds(8, 8), :], xm1.at[c, pl.ds(0, 8), :], (b, right)),
             (spd.at[c, CZ], spd.at[c, 0], (up, t)),
             (spd.at[c, pl.ds(1, 2)], spd.at[c, pl.ds(1 + CZ, 2)], (down, t)),
-            (first_x, xp16.at[c, pl.ds(8, 8), :], (b, left)),
-            (second_x, xp17.at[c], (b, left)),
-            (last_x, xm1.at[c, pl.ds(0, 8), :], (b, right)),
-            (last_x, xm1.at[c, pl.ds(8, 8), :], (down, right)),
-            (first_x, xp16.at[c, pl.ds(0, 8), :], (up, left)),
-            (first_x, xp16.at[c, pl.ds(16, 8), :], (down, left)),
-        ]
-        for i, (src, dst, device) in enumerate(moves):
-            copy = remote(src, dst, sp_send.at[c, i], sp_recv.at[c, i], device)
-            copy.start()
-            spd_copies.append(copy)
-    for copy in spd_copies:
-        copy.wait()
-
-    @pl.when(at_bottom)
-    def _():
-        for c in range(3):
-            spd[c, 0] = jnp.zeros((CX, CY), F32)
-            xp16[c, 0:8, :] = nothing
-
-    @pl.when(at_top)
-    def _():
-        for c in range(3):
-            spd[c, 1 + CZ : 3 + CZ] = jnp.zeros((2, CX, CY), F32)
-            xm1[c, 8:16, :] = nothing
-            xp16[c, 16:24, :] = nothing
-
-    @pl.when(at_left)
-    def _():
-        for c in range(3):
-            xm1[c] = jnp.zeros((16, CY), F32)
-
-    @pl.when(at_right)
-    def _():
-        for c in range(3):
-            xp16[c] = jnp.zeros((24, CY), F32)
-            xp17[c] = nothing
+        ))
+        change = spd[c, 1 : 1 + CZ, 1, :] - first_x
+        across = across + change * change
+        crs[0, c] = last_x[0:1]
+        crs[1, c] = first_x[7:8]
+        crs[2, c] = first_x[0:1]
+    qst[...] = across
+    send_speed((
+        (qst, xq, (b, left)),
+        (crs.at[0], crn.at[0], (down, right)),
+        (crs.at[1], crn.at[1], (up, left)),
+        (crs.at[2], crn.at[2], (down, left)),
+    ))
 
     def squared(here, *others):
         total = jnp.zeros_like(here)
@@ -415,8 +415,59 @@
             total = total + change * change
         return total
 
+    def viscosity(i, edge):
+        squares = jnp.zeros((CX, CY), F32)
+        for c in range(3):
+            here = spd[c, i]
+            row = here if edge is None else xp16[c, edge : edge + 1, :]
+            squares = squares + squared(here, spd[c, i + 1], ahead_x(here, row), ahead_y(here))
+        visc[i] = visc_of(squares)
+
+    def pressure(z, edge):
+        here = spd[0, z + 1]
+        div = here - spd[0, z]
+        here = spd[1, z + 1]
+        div = div + (here - behind_x(here, here if edge is None else xm1[1, edge : edge + 1, :]))
+        here = spd[2, z + 1]
+        div = div + (here - behind_y(here))
+        pres[z] = -penalty_factor * div
+
+    lax.fori_loop(1, CZ, lambda i, carry: (viscosity(i, None), carry)[1], 0)
+    lax.fori_loop(1, CZ, lambda z, carry: (pressure(z, None), carry)[1], 0)
+
+    for copy in spd_copies:
+        copy.wait()
+    for c in range(3):
+        xm1[c, 8:9, :] = crn[0, c]
+        xp16[c, 7:8, :] = crn[1, c]
+        xp16[c, 16:17, :] = crn[2, c]
+
+    @pl.when(at_bottom)
+    def _():
+        for c in range(3):
+            spd[c, 0] = jnp.zeros((CX, CY), F32)
+            xp16[c, 0:8, :] = nothing
+
+    @pl.when(at_top)
+    def _():
+        for c in range(3):
+            spd[c, 1 + CZ : 3 + CZ] = jnp.zeros((2, CX, CY), F32)
+            xm1[c, 8:16, :] = nothing
+            xp16[c, 16:24, :] = nothing
+
+    @pl.when(at_left)
+    def _():
+        for c in range(3):
+            xm1[c] = jnp.zeros((16, CY), F32)
+
+    @pl.when(at_right)
+    def _():
+        for c in range(3):
+            xp16[c] = jnp.zeros((24, CY), F32)
+
     squares_m = jnp.zeros((CZ, CY), F32)
-    squares_p = jnp.zeros((CZ, CY), F32)
+    squares_l = jnp.zeros((CZ, CY), F32)
+    squares_p = xq[...]
     for c in range(3):
         whole = xm1[c]
         here = whole[0:8]
@@ -425,55 +476,52 @@
         whole = xp16[c]
         here = whole[8:16]
         above = pltpu.roll(whole, 23, 0)[8:16]
-        squares_p = squares_p + squared(here, above, xp17[c], ahead_y(here))
-    visc_m = jnp.where(at_left, 0.0, visc_of(squares_m))
-    visc_p = jnp.where(at_right, 0.0, visc_of(squares_p))
-    plane[0, 0:8, :] = visc_m
-    plane[0, 8:16, :] = visc_p
+        squares_p = squares_p + squared(here, above, ahead_y(here))
+        last = plane[c, 8:16, :]
+        above = ahead_x(last, spd[c, 1 + CZ, CX - 1 : CX, :])
+        squares_l = squares_l + squared(last, above, here, ahead_y(last))
+    side[0:8, :] = jnp.where(at_left, 0.0, visc_of(squares_m))
+    side[8:16, :] = jnp.where(at_right, 0.0, visc_of(squares_p))
     here = xp16[0]
     div = here[8:16] - pltpu.roll(here, 1, 0)[8:16]
-    div = div + (xp16[1, 8:16, :] - plane[1, 16:24, :])
+    div = div + (xp16[1, 8:16, :] - plane[1, 8:16, :])
     here = xp16[2, 8:16, :]
     div = div + (here - behind_y(here))
-    plane[0, 16:24, :] = jnp.where(at_right, 0.0, -penalty_factor * div)
-
-    def viscosity(i, carry):
-        squares = jnp.zeros((CX, CY), F32)
-        for c in range(3):
-            here = spd[c, i]
-            edge = xp16[c, pl.ds(i + 7, 1), :]
-            squares = squares + squared(here, spd[c, i + 1], ahead_x(here, edge), ahead_y(here))
-        z = i - 1
-        inside = ((z >= 0) | jnp.logical_not(at_bottom)) & ((z < CZ) | jnp.logical_not(at_top))
-        visc[i] = jnp.where(inside, visc_of(squares), 0.0)
-        return carry
-
-    lax.fori_loop(0, CZ + 2, viscosity, 0)
-
-    def pressure(z, carry):
-        here = spd[0, z + 1]
-        div = here - spd[0, z]
-        here = spd[1, z + 1]
-        div = div + (here - behind_x(here, xm1[1, pl.ds(z, 1), :]))
-        here = spd[2, z + 1]
-        div = div + (here - behind_y(here))
-        inside = (z < CZ) | jnp.logical_not(at_top)
-        pres[z] = jnp.where(inside, -penalty_factor * div, 0.0)
-        return carry
-
-    lax.fori_loop(0, CZ + 1, pressure, 0)
+    side[16:24, :] = jnp.where(at_right, 0.0, -penalty_factor * div)
+    here = plane[0, 0:8, :]
+    div = here - behind_x(here, spd[0, 0, 0:1, :])
+    div = div + (plane[1, 0:8, :] - xm1[1, 0:8, :])
+    here = plane[2, 0:8, :]
+    div = div + (here - behind_y(here))
+
+    viscosity(0, 7)
+    viscosity(CZ, 15)
+    viscosity(CZ + 1, 16)
+    pressure(0, 0)
+    pressure(CZ, 8)
+    visc[1 : 1 + CZ, CX - 1, :] = visc_of(squares_l)
+    pres[0:CZ, 0, :] = -penalty_factor * div
+
+    @pl.when(at_bottom)
+    def _():
+        visc[0] = jnp.zeros((CX, CY), F32)
+
+    @pl.when(at_top)
+    def _():
+        visc[CZ + 1] = jnp.zeros((CX, CY), F32)
+        pres[CZ] = jnp.zeros((CX, CY), F32)
 
     def update(z, carry):
         v = visc[z + 1]
         line = pl.ds(z, 1)
-        v_next = (visc[z + 2], ahead_x(v, plane[0, pl.ds(z + 8, 1), :]), ahead_y(v))
-        v_prev = (visc[z], behind_x(v, plane[0, line, :]), behind_y(v))
+        v_next = (visc[z + 2], ahead_x(v, side[pl.ds(z + 8, 1), :]), ahead_y(v))
+        v_prev = (visc[z], behind_x(v, side[line, :]), behind_y(v))
         forward = [0.5 * (v + other) for other in v_next]
         backward = [0.5 * (v + other) for other in v_prev]
         density = kmass[z] / vol[z]
         bottom = forward[0] + backward[0] + forward[1] + backward[1] + forward[2] + backward[2] + density
         p = pres[z]
-        p_next = (pres[z + 1], ahead_x(p, plane[0, pl.ds(z + 16, 1), :]), ahead_y(p))
+        p_next = (pres[z + 1], ahead_x(p, side[pl.ds(z + 16, 1), :]), ahead_y(p))
         for c in range(3):
             here = spd[c, z + 1]
             top = forward[0] * spd[c, z + 2] + backward[0] * spd[c, z]
@@ -492,19 +540,36 @@
     regrid_out.wait()
 
 
+def store(regrid_ref, vel_ref, regrid_hbm, vel_hbm, sem):
+    copies = [
+        pltpu.make_async_copy(regrid_ref, regrid_hbm, sem.at[0]),
+        pltpu.make_async_copy(vel_ref, vel_hbm, sem.at[1]),
+    ]
+    for copy in copies:
+        copy.start()
+    for copy in copies:
+        copy.wait()
+
+
 def shards(
     displacement, old_mass, old_momentum, intersection_fraction, entry_order, target_owner,
     target_block, kept_mass, kept_momentum, surface_panels, panel_ids, contact_flags,
 ):
     grid = jax.ShapeDtypeStruct((3, CZ, CX, CY), F32)
-    hbm, vmem = pl.BlockSpec(memory_space=pl.ANY), pl.BlockSpec(memory_space=pltpu.VMEM)
+    hbm, vmem = pl.BlockSpec(memory_space=pltpu.HBM), pl.BlockSpec(memory_space=pltpu.VMEM)
     dma = pltpu.SemaphoreType.DMA
-    return pl.pallas_call(
+    regridded, velocity = pl.pallas_call(
         kernel,
-        out_shape=(grid, grid),
-        in_specs=[hbm, hbm, hbm, hbm, vmem, vmem, vmem, hbm, hbm, vmem, vmem, vmem],
-        out_specs=(hbm, vmem),
+        out_shape=(pltpu.VMEM(grid.shape, F32), pltpu.VMEM(grid.shape, F32)),
+        in_specs=[hbm] * 12,
+        out_specs=(vmem, vmem),
         scratch_shapes=[
+            pltpu.VMEM((1, OV), jnp.int32),
+            pltpu.VMEM((1, OV), jnp.int32),
+            pltpu.VMEM((1, OV), jnp.int32),
+            pltpu.VMEM((3, 4, 128), F32),
+            pltpu.VMEM((4, CX), jnp.int32),
+            pltpu.VMEM((4, CX), jnp.int32),
             pltpu.VMEM((3, CZ + 6, 32, CY), F32),
             pltpu.VMEM((3, CZ + 6, 32, CY), F32),
             pltpu.VMEM((COMPS, NBLK, 128), F32),
@@ -519,24 +584,29 @@
             pltpu.VMEM((N_TILE, 1, 128), F32),
             pltpu.VMEM((N_TILE, 1, 128), F32),
             pltpu.VMEM((NBLK, RROWS), BF16),
-            pltpu.VMEM((2, 72, CY), F32),
-            pltpu.VMEM((72, CY), F32),
-            pltpu.VMEM((72, CY), F32),
-            pltpu.VMEM((4, 16, CY), F32),
-            pltpu.VMEM((4, 16, CY), F32),
+            pltpu.VMEM((2, 8 * len(PLANES), CY), F32),
+            pltpu.VMEM((8 * len(PLANES), CY), F32),
+            pltpu.VMEM((8 * len(PLANES), CY), F32),
+            pltpu.VMEM((4, len(LINES), 1, CY), F32),
+            pltpu.VMEM((4, len(LINES), 1, CY), F32),
             pltpu.VMEM((N_TILE, 3, 4, 128), F32),
             pltpu.VMEM((3, CX, CY), F32),
             pltpu.VMEM((3, CZ + 3, CX, CY), F32),
-            pltpu.VMEM((3, 24, CY), F32),
+            pltpu.VMEM((3, 16, CY), F32),
             pltpu.VMEM((3, 16, CY), F32),
             pltpu.VMEM((3, 24, CY), F32),
-            pltpu.VMEM((3, 8, CY), F32),
+            pltpu.VMEM((8, CY), F32),
+            pltpu.VMEM((8, CY), F32),
+            pltpu.VMEM((3, 3, 1, CY), F32),
+            pltpu.VMEM((3, 3, 1, CY), F32),
+            pltpu.VMEM((24, CY), F32),
             pltpu.VMEM((CZ + 2, CX, CY), F32),
             pltpu.VMEM((CZ + 1, CX, CY), F32),
             dma((6,)),
+            dma((6,)),
             dma((1,)),
             dma((COMPS,)),
-            dma((COMPS,)),
+            dma((COMPS - 1 + len(PARTS),)),
             dma,
             dma,
             dma((8,)),
@@ -545,26 +615,39 @@
             dma((TY - 1,)),
             dma((TX - 1,)),
             dma((TX - 1,)),
-            dma((3, 8)),
-            dma((3, 8)),
+            dma((16,)),
+            dma((16,)),
         ],
         compiler_params=pltpu.CompilerParams(
             collective_id=0, has_side_effects=True, vmem_limit_bytes=48 * 2**20
         ),
     )(
-        displacement,
-        old_mass,
-        old_momentum.transpose(1, 0, 2),
-        intersection_fraction,
-        entry_order,
-        target_owner.reshape(1, OV),
-        target_block.reshape(1, OV),
-        kept_mass,
-        kept_momentum,
-        surface_panels.transpose(1, 0, 2),
-        panel_ids[0].T,
-        contact_flags[0].T,
+        *(
+            pltpu.with_memory_space_constraint(value, pltpu.HBM)
+            for value in (
+                displacement,
+                old_mass,
+                old_momentum.transpose(1, 0, 2),
+                intersection_fraction,
+                entry_order,
+                target_owner.reshape(1, OV),
+                target_block.reshape(1, OV),
+                kept_mass,
+                kept_momentum,
+                surface_panels.transpose(1, 0, 2),
+                panel_ids[0].T,
+                contact_flags[0].T,
+            )
+        )
     )
+    return pl.pallas_call(
+        store,
+        out_shape=(grid, grid),
+        in_specs=[vmem, vmem],
+        out_specs=(hbm, hbm),
+        scratch_shapes=[dma((2,))],
+        compiler_params=pltpu.CompilerParams(vmem_limit_bytes=2**20),
+    )(*(pltpu.with_memory_space_constraint(value, pltpu.VMEM) for value in (regridded, velocity)))
 
 
 def solution(mesh):

time: 101 us -> 85.9 us (0.85)
  local copies, waits for them, and re-layouts: 11.4 us -> 0 us
  Pallas kernels: 88.6 us -> 85.1 us
    unnamed x26 -> x0, local copies, waits for them, and re-layouts: 11.4 us -> none
    pallas_call x1 -> x2, Pallas kernels: 88.6 us -> 85.1 us  [the longest x1 84 us: shards(): pl.pallas_call(kernel, out_shape=(pltpu.VMEM(grid.shape, F32), pltpu.VMEM...]
where the time goes in v2:
time: 85.9 us; the launch traced here: 85.8 us
  Pallas kernels  85.1 us (99%)
    pallas_call x1, Pallas kernels, shards(): pl.pallas_call(kernel, out_shape=(pltpu.VMEM(grid.shape, F32), pltpu.VMEM...  84 us

profile of v2, /device:TPU:193, one launch (start us, length us, event | category | flops | bytes accessed | tf_op | source)
XLA Modules:
  0.0 85.8 jit_solution(15188878345268142753)
XLA Ops:
  0.6 84.0 %shard_map.131 = (f32[3,8,16,512]{3,2,1,0:T(8,128)S(1)}, f32[3,8,16,512]{3,2,1,0:T(8,128)S(1)}) custom-call(f32[3,8,16,512]{3,2,1,0:T(8,128)} %disp_hbm.1, f32[512,128]{1,0:T(8,128)} %mass_hbm.1, f32[3,512,128]{2,1,0:T(8,128)} %bitcast.10, f32[512,128]{1,0:T(8,128)} %frac_hbm.1, s32[1,1024]{1,0:T(1,128)} %order_hbm.1, s32[1,1024]{1,0:T(1,128)} %bitcast.12, ...), custom_call_target="tpu_custom_call" | custom-call | tf_op jit(solution)/shard_map/pallas_call | solution.py:561
  84.6 1.2 %shard_map.132 = (f32[3,8,16,512]{3,2,1,0:T(8,128)}, f32[3,8,16,512]{3,2,1,0:T(8,128)}) custom-call(f32[3,8,16,512]{3,2,1,0:T(8,128)S(1)} %get-tuple-element.4.regrid_ref, f32[3,8,16,512]{3,2,1,0:T(8,128)S(1)} %get-tuple-element.5.vel_ref), custom_call_target="tpu_custom_call" | custom-call | tf_op jit(solution)/shard_map/pallas_call | solution.py:643

commit v3 on v2

--- a/solution.py
+++ b/solution.py
@@ -71,9 +71,9 @@
     kmass_hbm, kmom_hbm, panels_hbm, pids_hbm, flags_hbm,
     regrid_ref, vel_ref,
     order_ref, owner_ref, block_ref, panels_ref, pids_ref, flags_ref,
-    ext, s1, old, frac, kmass, kmom, vol, sel_src, table, send, recv, ids_send, ids_recv,
+    ext, s1, old, frac, kmass, kmom, vol, sel_src, table, send, mid, recv, ids_send, ids_mid, ids_recv,
     sel_dst, xst, xhl, xhr, cst, chl, pans, trac, spd, plane, xm1, xp16, qst, xq, crs, crn, side, visc, pres,
-    small_sem, load_sem, out_sem, a2a_send, a2a_recv, ids_ssem, ids_rsem, dh_send, dh_recv,
+    small_sem, load_sem, out_sem, a2a_send, a2a_recv, mid_recv, fwd_send, ids_ssem, ids_rsem, im_send, im_recv, dh_send, dh_recv,
     py_send, py_recv, px_send, px_recv, sp_send, sp_recv,
 ):
     b = lax.axis_index("band")
@@ -86,10 +86,29 @@
         return ((tx + k // TY) % TX) * TY + (ty + k % TY) % TY
 
     barrier = pltpu.get_barrier_semaphore()
-    partners = [(b, peer(k)) for k in range(1, N_TILE)]
-    partners += [(up, t), (down, t), (up, right), (up, left), (down, right), (down, left)]
+    partners = [(b, peer(j)) for j in range(1, TY)] + [(b, peer(TY * i)) for i in range(1, TX)]
     for partner in partners:
         pl.semaphore_signal(barrier, inc=1, device_id=partner, device_id_type=MESH)
+    at_left, at_right = t == 0, t == N_TILE - 1
+    at_bottom, at_top = b == 0, b == N_BAND - 1
+
+    def there(dz, dx):
+        z_end = at_top if dz > 0 else at_bottom if dz < 0 else False
+        x_end = at_right if dx > 0 else at_left if dx < 0 else False
+        return jnp.logical_not(jnp.logical_or(z_end, x_end))
+
+    def neighbour(dz, dx):
+        return (up if dz > 0 else down if dz < 0 else b, right if dx > 0 else left if dx < 0 else t)
+
+    around = [(dz, dx) for dz in (-1, 0, 1) for dx in (-1, 0, 1) if (dz, dx) != (0, 0)]
+    greeted = len(partners)
+    for way in around:
+
+        @pl.when(there(*way))
+        def _():
+            pl.semaphore_signal(barrier, inc=1, device_id=neighbour(*way), device_id_type=MESH)
+
+        greeted = greeted + there(*way).astype(jnp.int32)
 
     small = [(owner_hbm, owner_ref), (order_hbm, order_ref), (block_hbm, block_ref),
              (panels_hbm, panels_ref), (pids_hbm, pids_ref), (flags_hbm, flags_ref)]
@@ -120,36 +139,6 @@
     for copy in small:
         copy.wait()
     pans[ty] = panels_ref[...]
-
-    pl.semaphore_wait(barrier, len(partners))
-
-    def remote(src, dst, ssem, rsem, device):
-        return pltpu.make_async_remote_copy(
-            src_ref=src, dst_ref=dst, send_sem=ssem, recv_sem=rsem, device_id=device, device_id_type=MESH
-        )
-
-    disp_copies = [
-        remote(xst.at[0], xhl, dh_send.at[0], dh_recv.at[0], (b, right)),
-        remote(xst.at[1], xhr, dh_send.at[1], dh_recv.at[1], (b, left)),
-        remote(disp_hbm.at[:, pl.ds(CZ - 3, 3)], ext.at[:, pl.ds(0, 3), pl.ds(TOP, CX), :],
-               dh_send.at[2], dh_recv.at[2], (up, t)),
-        remote(disp_hbm.at[:, pl.ds(0, 3)], ext.at[:, pl.ds(3 + CZ, 3), pl.ds(TOP, CX), :],
-               dh_send.at[3], dh_recv.at[3], (down, t)),
-    ]
-    for corner in range(4):
-        sz, sx = corner // 2, corner % 2
-        disp_copies.append(
-            remote(cst.at[corner], chl.at[corner], dh_send.at[4 + corner], dh_recv.at[4 + corner],
-                   (up if sz else down, right if sx else left))
-        )
-    for copy in disp_copies:
-        copy.start()
-    panel_y = [
-        remote(pans.at[ty], pans.at[ty], py_send.at[i - 1], py_recv.at[i - 1], (b, tx * TY + (ty + i) % TY))
-        for i in range(1, TY)
-    ]
-    for copy in panel_y:
-        copy.start()
 
     owner = owner_ref[...]
     column = iota((N_TILE, 1), 0)
@@ -186,10 +175,61 @@
         ids_send[k] = ids[k : k + 1, :]
     ids_recv[0] = ids[0:1, :]
 
-    ids_copies = [
-        remote(ids_send.at[k], ids_recv.at[k], ids_ssem, ids_rsem, (b, peer(k))) for k in range(1, N_TILE)
+
+    pl.semaphore_wait(barrier, greeted)
+
+    def remote(src, dst, ssem, rsem, device):
+        return pltpu.make_async_remote_copy(
+            src_ref=src, dst_ref=dst, send_sem=ssem, recv_sem=rsem, device_id=device, device_id_type=MESH
+        )
+
+    class Shift:
+        def __init__(self, src, dst, ssem, rsem, dz, dx):
+            self.copy = remote(src, dst, ssem, rsem, neighbour(dz, dx))
+            self.goes, self.comes = there(dz, dx), there(-dz, -dx)
+
+        def start(self):
+            pl.when(self.goes)(self.copy.start)
+
+        def wait(self):
+            pl.when(self.goes)(self.copy.wait_send)
+            pl.when(self.comes)(self.copy.wait_recv)
+
+    disp_copies = [
+        Shift(xst.at[0], xhl, dh_send.at[0], dh_recv.at[0], 0, 1),
+        Shift(xst.at[1], xhr, dh_send.at[1], dh_recv.at[1], 0, -1),
+        Shift(disp_hbm.at[:, pl.ds(CZ - 3, 3)], ext.at[:, pl.ds(0, 3), pl.ds(TOP, CX), :],
+              dh_send.at[2], dh_recv.at[2], 1, 0),
+        Shift(disp_hbm.at[:, pl.ds(0, 3)], ext.at[:, pl.ds(3 + CZ, 3), pl.ds(TOP, CX), :],
+              dh_send.at[3], dh_recv.at[3], -1, 0),
     ]
-
+    for corner in range(4):
+        sz, sx = corner // 2, corner % 2
+        disp_copies.append(
+            Shift(cst.at[corner], chl.at[corner], dh_send.at[4 + corner], dh_recv.at[4 + corner],
+                  1 if sz else -1, 1 if sx else -1)
+        )
+    for copy in disp_copies:
+        copy.start()
+    panel_y = [
+        remote(pans.at[ty], pans.at[ty], py_send.at[i - 1], py_recv.at[i - 1], (b, tx * TY + (ty + i) % TY))
+        for i in range(1, TY)
+    ]
+    for copy in panel_y:
+        copy.start()
+
+    def column(j):
+        return (b, peer(j))
+
+    def across(i):
+        return (b, peer(TY * i))
+
+    ids_copies = [remote(ids_send.at[j], ids_recv.at[j], ids_ssem, ids_rsem, column(j)) for j in range(1, TY)]
+    for i in range(1, TX):
+        ids_copies += [
+            remote(ids_send.at[TY * i], ids_recv.at[TY * i], ids_ssem, ids_rsem, across(i)),
+            remote(ids_send.at[pl.ds(TY * i + 1, TY - 1)], ids_mid.at[i - 1], ids_ssem, im_recv.at[i - 1], across(i)),
+        ]
     for copy in ids_copies:
         copy.start()
 
@@ -207,22 +247,37 @@
         table[NBLK : 2 * NBLK, 0:128] = high
         table[NBLK : 2 * NBLK, 128:256] = low
 
-    def rows_copy(c, k):
+    def rows_copy(src, c, k, ssem, device):
         return remote(
-            send.at[c, pl.ds(CAP * k, CAP), :], recv.at[c, pl.ds(slot_row(k), CAP), :],
-            a2a_send.at[c], a2a_recv.at[c + (c // 3) * (k // 12)], (b, peer(k)),
+            src, recv.at[c, pl.ds(slot_row(k), CAP), :], ssem, a2a_recv.at[c + (c // 3) * (k // 12)], device
         )
+
+    def bundle_copy(c, i):
+        src = send.at[c, pl.ds(CAP * (TY * i + 1), CAP * (TY - 1)), :]
+        return remote(src, mid.at[c, i - 1], a2a_send.at[c], mid_recv.at[c, i - 1], across(i))
 
     def dispatch(c, g):
         both = jnp.dot(sel_src[g], table[...], preferred_element_type=F32)
         rows = both[:, 0:128] + both[:, 128:256]
         send[c, pl.ds(ROWS * g, ROWS), :] = rows
+        i = g // 2
         if g == 0:
             recv[c, 0:CAP, :] = rows[0:CAP]
-        for j in range(GROUP):
-            k = GROUP * g + j
-            if k:
-                rows_copy(c, k).start()
+        elif g % 2 == 0:
+            k = TY * i
+            rows_copy(send.at[c, pl.ds(CAP * k, CAP), :], c, k, a2a_send.at[c], across(i)).start()
+        if i == 0:
+            for j in range(max(GROUP * g, 1), GROUP * (g + 1)):
+                rows_copy(send.at[c, pl.ds(CAP * j, CAP), :], c, j, a2a_send.at[c], column(j)).start()
+        elif g % 2 == 1:
+            bundle_copy(c, i).start()
+
+    def forward(c):
+        for i in range(1, TX):
+            bundle_copy(c, i).wait_recv()
+            for j in range(1, TY):
+                src = mid.at[c, i - 1, pl.ds(CAP * (j - 1), CAP), :]
+                rows_copy(src, c, TY * i + j, fwd_send.at[c], column(j)).start()
 
     fill_table(0)
     for g in range(GROUPS):
@@ -232,29 +287,32 @@
         sel_src[g] = jnp.where(hit, 1.0, 0.0).astype(BF16)
         dispatch(0, g)
 
-    for i, copy in enumerate(panel_y):
-        copy.wait()
-
-    panel_x = [
-        remote(pans.at[pl.ds(0, TY)], pans.at[pl.ds(TY * i, TY)], px_send.at[i - 1], px_recv.at[i - 1],
-               (b, ((tx + i) % TX) * TY + ty))
-        for i in range(1, TX)
-    ]
-    for copy in panel_x:
-        copy.start()
-
     def later(c, carry):
         fill_table(c)
         for g in range(GROUPS):
             dispatch(c, g)
         return carry
 
-    lax.fori_loop(1, COMPS, later, 0)
+    for copy in panel_y:
+        copy.wait()
+    panel_x = [
+        remote(pans.at[pl.ds(0, TY)], pans.at[pl.ds(TY * i, TY)], px_send.at[i - 1], px_recv.at[i - 1], across(i))
+        for i in range(1, TX)
+    ]
+    for copy in panel_x:
+        copy.start()
+    for i in range(1, TX):
+        ids_copies[TY - 1 + 2 * (i - 1) + 1].wait_recv()
+        for j in range(1, TY):
+            remote(ids_mid.at[i - 1, j - 1], ids_recv.at[TY * i + j], im_send, ids_rsem, column(j)).start()
+
+    lax.fori_loop(1, COMPS - 1, later, 0)
+    forward(0)
+    lax.fori_loop(COMPS - 1, COMPS, later, 0)
+    forward(1)
 
     for copy in disp_copies:
         copy.wait()
-    at_left, at_right = t == 0, t == N_TILE - 1
-    at_bottom, at_top = b == 0, b == N_BAND - 1
     nothing = jnp.zeros((8, CY), F32)
     for i, (c, d) in enumerate(PLANES):
         at = pl.ds(8 * i, 8)
@@ -312,10 +370,10 @@
         zi = z + 3
         own = pl.ds(TOP, CX)
         stretch = ext[0, zi + 1, own, :] - ext[0, zi - 1, own, :]
-        across = ext[1, zi]
-        across = pltpu.roll(across, 31, 0) - pltpu.roll(across, 1, 0)
+        wide = ext[1, zi]
+        wide = pltpu.roll(wide, 31, 0) - pltpu.roll(wide, 1, 0)
         along = ext[2, zi, own, :]
-        stretch = stretch + across[TOP : TOP + CX] + (ahead_y(along) - behind_y(along))
+        stretch = stretch + wide[TOP : TOP + CX] + (ahead_y(along) - behind_y(along))
         vol[z] = 1.0 + cell_fraction * (0.5 * stretch)
         return carry
 
@@ -337,6 +395,8 @@
             got = lax.dot_general(weight, high, tn, preferred_element_type=F32)
             got = got + lax.dot_general(weight, low, tn, preferred_element_type=F32)
             trac[c, :, 128 * yb : 128 * (yb + 1)] = got
+
+    forward(2)
 
     bulk = (N_TILE - 1) * CAP
     pltpu.make_async_copy(ids_recv.at[pl.ds(1, N_TILE - 1)], ids_recv.at[pl.ds(1, N_TILE - 1)], ids_rsem).wait()
@@ -351,6 +411,8 @@
         for c in range(COMPS):
             recv[c, 128 * s + used : 128 * (s + 1), :] = jnp.zeros((128 - used, 128), F32)
 
+    forward(3)
+
     def arrived(c, first, last, sem):
         rows = CAP * (min(3 * last, N_TILE) - max(3 * first, 1))
         pltpu.make_async_copy(recv.at[c, pl.ds(0, rows)], recv.at[c, pl.ds(0, rows)], sem).wait()
@@ -375,12 +437,12 @@
     spd_copies = []
 
     def send_speed(moves):
-        for src, dst, device in moves:
+        for src, dst, dz, dx in moves:
             i = len(spd_copies)
-            spd_copies.append(remote(src, dst, sp_send.at[i], sp_recv.at[i], device))
+            spd_copies.append(Shift(src, dst, sp_send.at[i], sp_recv.at[i], dz, dx))
             spd_copies[-1].start()
 
-    across = jnp.zeros((CZ, CY), F32)
+    change_x = jnp.zeros((CZ, CY), F32)
     for c in range(3):
         for yb, more in enumerate(incoming(c + 1)):
             at = pl.ds(128 * yb, 128)
@@ -390,22 +452,22 @@
         plane[c, 0:8, :] = first_x
         plane[c, 8:16, :] = last_x
         send_speed((
-            (plane.at[c, pl.ds(0, 8), :], xp16.at[c, pl.ds(8, 8), :], (b, left)),
-            (plane.at[c, pl.ds(8, 8), :], xm1.at[c, pl.ds(0, 8), :], (b, right)),
-            (spd.at[c, CZ], spd.at[c, 0], (up, t)),
-            (spd.at[c, pl.ds(1, 2)], spd.at[c, pl.ds(1 + CZ, 2)], (down, t)),
+            (plane.at[c, pl.ds(0, 8), :], xp16.at[c, pl.ds(8, 8), :], 0, -1),
+            (plane.at[c, pl.ds(8, 8), :], xm1.at[c, pl.ds(0, 8), :], 0, 1),
+            (spd.at[c, CZ], spd.at[c, 0], 1, 0),
+            (spd.at[c, pl.ds(1, 2)], spd.at[c, pl.ds(1 + CZ, 2)], -1, 0),
         ))
         change = spd[c, 1 : 1 + CZ, 1, :] - first_x
-        across = across + change * change
+        change_x = change_x + change * change
         crs[0, c] = last_x[0:1]
         crs[1, c] = first_x[7:8]
         crs[2, c] = first_x[0:1]
-    qst[...] = across
+    qst[...] = change_x
     send_speed((
-        (qst, xq, (b, left)),
-        (crs.at[0], crn.at[0], (down, right)),
-        (crs.at[1], crn.at[1], (up, left)),
-        (crs.at[2], crn.at[2], (down, left)),
+        (qst, xq, 0, -1),
+        (crs.at[0], crn.at[0], -1, 1),
+        (crs.at[1], crn.at[1], 1, -1),
+        (crs.at[2], crn.at[2], -1, -1),
     ))
 
     def squared(here, *others):
@@ -536,7 +598,9 @@
 
     for c in range(COMPS):
         pltpu.make_async_copy(send.at[c, pl.ds(0, bulk)], send.at[c, pl.ds(0, bulk)], a2a_send.at[c]).wait()
+        pltpu.make_async_copy(mid.at[c], mid.at[c], fwd_send.at[c]).wait()
     pltpu.make_async_copy(ids_send.at[pl.ds(1, N_TILE - 1)], ids_send.at[pl.ds(1, N_TILE - 1)], ids_ssem).wait()
+    pltpu.make_async_copy(ids_mid, ids_mid, im_send).wait()
     regrid_out.wait()
 
 
@@ -580,8 +644,10 @@
             pltpu.VMEM((GROUPS, ROWS, OV), BF16),
             pltpu.VMEM((2 * NBLK, 256), BF16),
             pltpu.VMEM((COMPS, N_TILE * CAP, 128), F32),
+            pltpu.VMEM((COMPS, TX - 1, CAP * (TY - 1), 128), F32),
             pltpu.VMEM((COMPS, RROWS, 128), F32),
             pltpu.VMEM((N_TILE, 1, 128), F32),
+            pltpu.VMEM((TX - 1, TY - 1, 1, 128), F32),
             pltpu.VMEM((N_TILE, 1, 128), F32),
             pltpu.VMEM((NBLK, RROWS), BF16),
             pltpu.VMEM((2, 8 * len(PLANES), CY), F32),
@@ -607,8 +673,12 @@
             dma((1,)),
             dma((COMPS,)),
             dma((COMPS - 1 + len(PARTS),)),
+            dma((COMPS, TX - 1)),
+            dma((COMPS,)),
             dma,
             dma,
+            dma,
+            dma((TX - 1,)),
             dma((8,)),
             dma((8,)),
             dma((TY - 1,)),

time: 85.9 us -> 83.4 us (0.971)
  the two profiles are of different devices: /device:TPU:193 before, /device:TPU:135 now
where the time goes in v3:
time: 83.4 us; the launch traced here: 83.2 us
  Pallas kernels  82.6 us (99%)
    pallas_call x1, Pallas kernels, shards(): pl.pallas_call(kernel, out_shape=(pltpu.VMEM(grid.shape, F32), pltpu.VMEM...  81.4 us

profile of v3, /device:TPU:135, one launch (start us, length us, event | category | flops | bytes accessed | tf_op | source)
XLA Modules:
  0.0 83.2 jit_solution(5220874834606542945)
XLA Ops:
  0.6 81.4 %shard_map.131 = (f32[3,8,16,512]{3,2,1,0:T(8,128)S(1)}, f32[3,8,16,512]{3,2,1,0:T(8,128)S(1)}) custom-call(f32[3,8,16,512]{3,2,1,0:T(8,128)} %disp_hbm.1, f32[512,128]{1,0:T(8,128)} %mass_hbm.1, f32[3,512,128]{2,1,0:T(8,128)} %bitcast.10, f32[512,128]{1,0:T(8,128)} %frac_hbm.1, s32[1,1024]{1,0:T(1,128)} %order_hbm.1, s32[1,1024]{1,0:T(1,128)} %bitcast.12, ...), custom_call_target="tpu_custom_call" | custom-call | tf_op jit(solution)/shard_map/pallas_call | solution.py:625
  82.1 1.2 %shard_map.132 = (f32[3,8,16,512]{3,2,1,0:T(8,128)}, f32[3,8,16,512]{3,2,1,0:T(8,128)}) custom-call(f32[3,8,16,512]{3,2,1,0:T(8,128)S(1)} %get-tuple-element.4.regrid_ref, f32[3,8,16,512]{3,2,1,0:T(8,128)S(1)} %get-tuple-element.5.vel_ref), custom_call_target="tpu_custom_call" | custom-call | tf_op jit(solution)/shard_map/pallas_call | solution.py:713

commit v4 on v3

--- a/solution.py
+++ b/solution.py
@@ -69,10 +69,10 @@
 def kernel(
     disp_hbm, mass_hbm, mom_hbm, frac_hbm, order_hbm, owner_hbm, block_hbm,
     kmass_hbm, kmom_hbm, panels_hbm, pids_hbm, flags_hbm,
-    regrid_ref, vel_ref,
+    regrid_ref, spd, xm1, xp16, side, visc, pres, dens, trac,
     order_ref, owner_ref, block_ref, panels_ref, pids_ref, flags_ref,
     ext, s1, old, frac, kmass, kmom, vol, sel_src, table, send, mid, recv, ids_send, ids_mid, ids_recv,
-    sel_dst, xst, xhl, xhr, cst, chl, pans, trac, spd, plane, xm1, xp16, qst, xq, crs, crn, side, visc, pres,
+    sel_dst, xst, xhl, xhr, cst, chl, pans, plane, qst, xq, crs, crn,
     small_sem, load_sem, out_sem, a2a_send, a2a_recv, mid_recv, fwd_send, ids_ssem, ids_rsem, im_send, im_recv, dh_send, dh_recv,
     py_send, py_recv, px_send, px_recv, sp_send, sp_recv,
 ):
@@ -83,7 +83,8 @@
     right, left = (t + 1) % N_TILE, (t + N_TILE - 1) % N_TILE
 
     def peer(k):
-        return ((tx + k // TY) % TX) * TY + (ty + k % TY) % TY
+        i = k // TY
+        return ((tx + (i ^ (i >> 1))) % TX) * TY + (ty + k % TY) % TY
 
     barrier = pltpu.get_barrier_semaphore()
     partners = [(b, peer(j)) for j in range(1, TY)] + [(b, peer(TY * i)) for i in range(1, TX)]
@@ -121,28 +122,15 @@
         pltpu.make_async_copy(kmass_hbm, kmass, load_sem.at[4]),
         pltpu.make_async_copy(kmom_hbm, kmom, load_sem.at[5]),
     ]
-    loads[0].start()
-    for copy in small + loads[1:]:
+    for copy in small + loads[1:4] + loads[:1] + loads[4:]:
         copy.start()
 
-    loads[0].wait()
-    for i, (c, d) in enumerate(PLANES):
-        at = pl.ds(8 * i, 8)
-        xst[0, at, :] = ext[c, 3:11, TOP + CX - d, :]
-        xst[1, at, :] = ext[c, 3:11, TOP + d - 1, :]
-    for corner in range(4):
-        sz, sx = corner // 2, corner % 2
-        for i, (c, dz, dx) in enumerate(LINES):
-            z = CZ - dz if sz else dz - 1
-            x = CX - dx if sx else dx - 1
-            cst[corner, i] = ext[c, 3 + z, pl.ds(TOP + x, 1), :]
     for copy in small:
         copy.wait()
-    pans[ty] = panels_ref[...]
-
     owner = owner_ref[...]
     column = iota((N_TILE, 1), 0)
-    column_dest = ((tx + column // TY) % TX) * TY + (ty + column % TY) % TY
+    steps = column // TY
+    column_dest = ((tx + (steps ^ (steps >> 1))) % TX) * TY + (ty + column % TY) % TY
     before = (iota((128, 128), 0) < iota((128, 128), 1)).astype(BF16)
     base = jnp.zeros((N_TILE, 1), F32)
     slots, names = [], []
@@ -157,6 +145,73 @@
     place = name * CAP + slot
     order = order_ref[...]
     code = (order // 2 + (order % 2) * NBLK + 1).astype(F32)
+
+
+    def remote(src, dst, ssem, rsem, device):
+        return pltpu.make_async_remote_copy(
+            src_ref=src, dst_ref=dst, send_sem=ssem, recv_sem=rsem, device_id=device, device_id_type=MESH
+        )
+
+    def column(j):
+        return (b, peer(j))
+
+    def across(i):
+        return (b, peer(TY * i))
+
+    for copy in loads[1:4]:
+        copy.wait()
+
+    def fill_table(c):
+        share = frac[...]
+        values = old[c]
+        one = share * values
+        high, low = split2(one)
+        table[0:NBLK, 0:128] = high
+        table[0:NBLK, 128:256] = low
+        high, low = split2((1.0 - share) * values)
+        table[NBLK : 2 * NBLK, 0:128] = high
+        table[NBLK : 2 * NBLK, 128:256] = low
+
+    def rows_copy(src, c, k, ssem, device):
+        return remote(
+            src, recv.at[c, pl.ds(slot_row(k), CAP), :], ssem, a2a_recv.at[c + (c // 3) * (k // 12)], device
+        )
+
+    def bundle_copy(c, i):
+        src = send.at[c, pl.ds(CAP * (TY * i + 1), CAP * (TY - 1)), :]
+        return remote(src, mid.at[c, i - 1], a2a_send.at[c], mid_recv.at[c, i - 1], across(i))
+
+    def dispatch(c, g):
+        both = jnp.dot(sel_src[g], table[...], preferred_element_type=F32)
+        rows = both[:, 0:128] + both[:, 128:256]
+        send[c, pl.ds(ROWS * g, ROWS), :] = rows
+        i = g // 2
+        if g == 0:
+            recv[c, 0:CAP, :] = rows[0:CAP]
+        elif g % 2 == 0:
+            k = TY * i
+            rows_copy(send.at[c, pl.ds(CAP * k, CAP), :], c, k, a2a_send.at[c], across(i)).start()
+        if i == 0:
+            for j in range(max(GROUP * g, 1), GROUP * (g + 1)):
+                rows_copy(send.at[c, pl.ds(CAP * j, CAP), :], c, j, a2a_send.at[c], column(j)).start()
+        elif g % 2 == 1:
+            bundle_copy(c, i).start()
+
+    def forward(c):
+        for i in range(1, TX):
+            bundle_copy(c, i).wait_recv()
+            for j in range(1, TY):
+                src = mid.at[c, i - 1, pl.ds(CAP * (j - 1), CAP), :]
+                rows_copy(src, c, TY * i + j, fwd_send.at[c], column(j)).start()
+
+    fill_table(0)
+    pl.semaphore_wait(barrier, greeted)
+    for g in range(GROUPS):
+        wanted = (ROWS * g + iota((ROWS, 1), 0)).astype(F32)
+        code_of = jnp.sum(jnp.where(place == wanted, code, 0.0), axis=1, keepdims=True)
+        hit = code_of.astype(jnp.int32) == iota((ROWS, OV), 1) + 1
+        sel_src[g] = jnp.where(hit, 1.0, 0.0).astype(BF16)
+        dispatch(0, g)
 
     block = block_ref[...]
     target = (block % 4) * 128 + block // 4 + 1
@@ -176,12 +231,27 @@
     ids_recv[0] = ids[0:1, :]
 
 
-    pl.semaphore_wait(barrier, greeted)
-
-    def remote(src, dst, ssem, rsem, device):
-        return pltpu.make_async_remote_copy(
-            src_ref=src, dst_ref=dst, send_sem=ssem, recv_sem=rsem, device_id=device, device_id_type=MESH
-        )
+    ids_copies = [remote(ids_send.at[j], ids_recv.at[j], ids_ssem, ids_rsem, column(j)) for j in range(1, TY)]
+    for i in range(1, TX):
+        ids_copies += [
+            remote(ids_send.at[TY * i], ids_recv.at[TY * i], ids_ssem, ids_rsem, across(i)),
+            remote(ids_send.at[pl.ds(TY * i + 1, TY - 1)], ids_mid.at[i - 1], ids_ssem, im_recv.at[i - 1], across(i)),
+        ]
+    for copy in ids_copies:
+        copy.start()
+
+    loads[0].wait()
+    for i, (c, d) in enumerate(PLANES):
+        at = pl.ds(8 * i, 8)
+        xst[0, at, :] = ext[c, 3:11, TOP + CX - d, :]
+        xst[1, at, :] = ext[c, 3:11, TOP + d - 1, :]
+    for corner in range(4):
+        sz, sx = corner // 2, corner % 2
+        for i, (c, dz, dx) in enumerate(LINES):
+            z = CZ - dz if sz else dz - 1
+            x = CX - dx if sx else dx - 1
+            cst[corner, i] = ext[c, 3 + z, pl.ds(TOP + x, 1), :]
+    pans[ty] = panels_ref[...]
 
     class Shift:
         def __init__(self, src, dst, ssem, rsem, dz, dx):
@@ -218,81 +288,13 @@
     for copy in panel_y:
         copy.start()
 
-    def column(j):
-        return (b, peer(j))
-
-    def across(i):
-        return (b, peer(TY * i))
-
-    ids_copies = [remote(ids_send.at[j], ids_recv.at[j], ids_ssem, ids_rsem, column(j)) for j in range(1, TY)]
-    for i in range(1, TX):
-        ids_copies += [
-            remote(ids_send.at[TY * i], ids_recv.at[TY * i], ids_ssem, ids_rsem, across(i)),
-            remote(ids_send.at[pl.ds(TY * i + 1, TY - 1)], ids_mid.at[i - 1], ids_ssem, im_recv.at[i - 1], across(i)),
-        ]
-    for copy in ids_copies:
-        copy.start()
-
-    for copy in loads[1:4]:
-        copy.wait()
-
-    def fill_table(c):
-        share = frac[...]
-        values = old[c]
-        one = share * values
-        high, low = split2(one)
-        table[0:NBLK, 0:128] = high
-        table[0:NBLK, 128:256] = low
-        high, low = split2((1.0 - share) * values)
-        table[NBLK : 2 * NBLK, 0:128] = high
-        table[NBLK : 2 * NBLK, 128:256] = low
-
-    def rows_copy(src, c, k, ssem, device):
-        return remote(
-            src, recv.at[c, pl.ds(slot_row(k), CAP), :], ssem, a2a_recv.at[c + (c // 3) * (k // 12)], device
-        )
-
-    def bundle_copy(c, i):
-        src = send.at[c, pl.ds(CAP * (TY * i + 1), CAP * (TY - 1)), :]
-        return remote(src, mid.at[c, i - 1], a2a_send.at[c], mid_recv.at[c, i - 1], across(i))
-
-    def dispatch(c, g):
-        both = jnp.dot(sel_src[g], table[...], preferred_element_type=F32)
-        rows = both[:, 0:128] + both[:, 128:256]
-        send[c, pl.ds(ROWS * g, ROWS), :] = rows
-        i = g // 2
-        if g == 0:
-            recv[c, 0:CAP, :] = rows[0:CAP]
-        elif g % 2 == 0:
-            k = TY * i
-            rows_copy(send.at[c, pl.ds(CAP * k, CAP), :], c, k, a2a_send.at[c], across(i)).start()
-        if i == 0:
-            for j in range(max(GROUP * g, 1), GROUP * (g + 1)):
-                rows_copy(send.at[c, pl.ds(CAP * j, CAP), :], c, j, a2a_send.at[c], column(j)).start()
-        elif g % 2 == 1:
-            bundle_copy(c, i).start()
-
-    def forward(c):
-        for i in range(1, TX):
-            bundle_copy(c, i).wait_recv()
-            for j in range(1, TY):
-                src = mid.at[c, i - 1, pl.ds(CAP * (j - 1), CAP), :]
-                rows_copy(src, c, TY * i + j, fwd_send.at[c], column(j)).start()
-
-    fill_table(0)
-    for g in range(GROUPS):
-        wanted = (ROWS * g + iota((ROWS, 1), 0)).astype(F32)
-        code_of = jnp.sum(jnp.where(place == wanted, code, 0.0), axis=1, keepdims=True)
-        hit = code_of.astype(jnp.int32) == iota((ROWS, OV), 1) + 1
-        sel_src[g] = jnp.where(hit, 1.0, 0.0).astype(BF16)
-        dispatch(0, g)
-
     def later(c, carry):
         fill_table(c)
         for g in range(GROUPS):
             dispatch(c, g)
         return carry
 
+    lax.fori_loop(1, COMPS - 1, later, 0)
     for copy in panel_y:
         copy.wait()
     panel_x = [
@@ -306,7 +308,6 @@
         for j in range(1, TY):
             remote(ids_mid.at[i - 1, j - 1], ids_recv.at[TY * i + j], im_send, ids_rsem, column(j)).start()
 
-    lax.fori_loop(1, COMPS - 1, later, 0)
     forward(0)
     lax.fori_loop(COMPS - 1, COMPS, later, 0)
     forward(1)
@@ -383,7 +384,8 @@
         copy.wait()
     source = iota((N_TILE * 4, CX), 0)
     member = source // 4
-    panel = ((tx + TX - member // TY) % TX) * (TY * 4) + (member % TY) * 4 + source % 4
+    steps = member // TY
+    panel = ((tx + TX - (steps ^ (steps >> 1))) % TX) * (TY * 4) + (member % TY) * 4 + source % 4
     for yb in range(CY // 128):
         chosen = (panel == pids_ref[yb : yb + 1, :]) & (flags_ref[yb : yb + 1, :] != 0)
         chosen = jnp.where(chosen, 1.0, 0.0)
@@ -432,7 +434,9 @@
         copy.wait()
     for yb, more in enumerate(incoming(0)):
         at = pl.ds(128 * yb, 128)
-        kmass[:, :, at] = kmass[:, :, at] + more
+        mass = kmass[:, :, at] + more
+        dens[:, :, at] = mass / vol[:, :, at]
+        kmass[:, :, at] = 1.0 / mass
 
     spd_copies = []
 
@@ -446,7 +450,7 @@
     for c in range(3):
         for yb, more in enumerate(incoming(c + 1)):
             at = pl.ds(128 * yb, 128)
-            spd[c, 1 : 1 + CZ, :, at] = (kmom[c, :, :, at] + more) / kmass[:, :, at]
+            spd[c, 1 : 1 + CZ, :, at] = (kmom[c, :, :, at] + more) * kmass[:, :, at]
         first_x = spd[c, 1 : 1 + CZ, 0, :]
         last_x = spd[c, 1 : 1 + CZ, CX - 1, :]
         plane[c, 0:8, :] = first_x
@@ -573,6 +577,18 @@
         visc[CZ + 1] = jnp.zeros((CX, CY), F32)
         pres[CZ] = jnp.zeros((CX, CY), F32)
 
+    for c in range(COMPS):
+        pltpu.make_async_copy(send.at[c, pl.ds(0, bulk)], send.at[c, pl.ds(0, bulk)], a2a_send.at[c]).wait()
+        pltpu.make_async_copy(mid.at[c], mid.at[c], fwd_send.at[c]).wait()
+    pltpu.make_async_copy(ids_send.at[pl.ds(1, N_TILE - 1)], ids_send.at[pl.ds(1, N_TILE - 1)], ids_ssem).wait()
+    pltpu.make_async_copy(ids_mid, ids_mid, im_send).wait()
+    regrid_out.wait()
+
+
+def finish(regrid_ref, spd, xm1, xp16, side, visc, pres, dens, trac, regrid_hbm, vel_hbm, vel, sem):
+    regrid_out = pltpu.make_async_copy(regrid_ref, regrid_hbm, sem.at[CZ])
+    regrid_out.start()
+
     def update(z, carry):
         v = visc[z + 1]
         line = pl.ds(z, 1)
@@ -580,7 +596,7 @@
         v_prev = (visc[z], behind_x(v, side[line, :]), behind_y(v))
         forward = [0.5 * (v + other) for other in v_next]
         backward = [0.5 * (v + other) for other in v_prev]
-        density = kmass[z] / vol[z]
+        density = dens[z]
         bottom = forward[0] + backward[0] + forward[1] + backward[1] + forward[2] + backward[2] + density
         p = pres[z]
         p_next = (pres[z + 1], ahead_x(p, side[pl.ds(z + 16, 1), :]), ahead_y(p))
@@ -591,28 +607,14 @@
             top = top + backward[1] * behind_x(here, xm1[c, line, :])
             top = top + forward[2] * ahead_y(here) + backward[2] * behind_y(here)
             top = top - (p_next[c] - p) + trac[c] + density * here
-            vel_ref[c, z] = top / bottom
+            vel[c, z] = top / bottom
+        pltpu.make_async_copy(vel.at[:, z], vel_hbm.at[:, z], sem.at[z]).start()
         return carry
 
     lax.fori_loop(0, CZ, update, 0)
-
-    for c in range(COMPS):
-        pltpu.make_async_copy(send.at[c, pl.ds(0, bulk)], send.at[c, pl.ds(0, bulk)], a2a_send.at[c]).wait()
-        pltpu.make_async_copy(mid.at[c], mid.at[c], fwd_send.at[c]).wait()
-    pltpu.make_async_copy(ids_send.at[pl.ds(1, N_TILE - 1)], ids_send.at[pl.ds(1, N_TILE - 1)], ids_ssem).wait()
-    pltpu.make_async_copy(ids_mid, ids_mid, im_send).wait()
+    for z in range(CZ):
+        pltpu.make_async_copy(vel.at[:, z], vel_hbm.at[:, z], sem.at[z]).wait()
     regrid_out.wait()
-
-
-def store(regrid_ref, vel_ref, regrid_hbm, vel_hbm, sem):
-    copies = [
-        pltpu.make_async_copy(regrid_ref, regrid_hbm, sem.at[0]),
-        pltpu.make_async_copy(vel_ref, vel_hbm, sem.at[1]),
-    ]
-    for copy in copies:
-        copy.start()
-    for copy in copies:
-        copy.wait()
 
 
 def shards(
@@ -622,11 +624,22 @@
     grid = jax.ShapeDtypeStruct((3, CZ, CX, CY), F32)
     hbm, vmem = pl.BlockSpec(memory_space=pltpu.HBM), pl.BlockSpec(memory_space=pltpu.VMEM)
     dma = pltpu.SemaphoreType.DMA
-    regridded, velocity = pl.pallas_call(
+    parts = (
+        (3, CZ, CX, CY),
+        (3, CZ + 3, CX, CY),
+        (3, 16, CY),
+        (3, 24, CY),
+        (24, CY),
+        (CZ + 2, CX, CY),
+        (CZ + 1, CX, CY),
+        (CZ, CX, CY),
+        (3, CX, CY),
+    )
+    fields = pl.pallas_call(
         kernel,
-        out_shape=(pltpu.VMEM(grid.shape, F32), pltpu.VMEM(grid.shape, F32)),
+        out_shape=[pltpu.VMEM(part, F32) for part in parts],
         in_specs=[hbm] * 12,
-        out_specs=(vmem, vmem),
+        out_specs=[vmem] * len(parts),
         scratch_shapes=[
             pltpu.VMEM((1, OV), jnp.int32),
             pltpu.VMEM((1, OV), jnp.int32),
@@ -656,18 +669,11 @@
             pltpu.VMEM((4, len(LINES), 1, CY), F32),
             pltpu.VMEM((4, len(LINES), 1, CY), F32),
             pltpu.VMEM((N_TILE, 3, 4, 128), F32),
-            pltpu.VMEM((3, CX, CY), F32),
-            pltpu.VMEM((3, CZ + 3, CX, CY), F32),
             pltpu.VMEM((3, 16, CY), F32),
-            pltpu.VMEM((3, 16, CY), F32),
-            pltpu.VMEM((3, 24, CY), F32),
             pltpu.VMEM((8, CY), F32),
             pltpu.VMEM((8, CY), F32),
             pltpu.VMEM((3, 3, 1, CY), F32),
             pltpu.VMEM((3, 3, 1, CY), F32),
-            pltpu.VMEM((24, CY), F32),
-            pltpu.VMEM((CZ + 2, CX, CY), F32),
-            pltpu.VMEM((CZ + 1, CX, CY), F32),
             dma((6,)),
             dma((6,)),
             dma((1,)),
@@ -711,13 +717,13 @@
         )
     )
     return pl.pallas_call(
-        store,
+        finish,
         out_shape=(grid, grid),
-        in_specs=[vmem, vmem],
+        in_specs=[vmem] * len(parts),
         out_specs=(hbm, hbm),
-        scratch_shapes=[dma((2,))],
-        compiler_params=pltpu.CompilerParams(vmem_limit_bytes=2**20),
-    )(*(pltpu.with_memory_space_constraint(value, pltpu.VMEM) for value in (regridded, velocity)))
+        scratch_shapes=[pltpu.VMEM(grid.shape, F32), dma((CZ + 1,))],
+        compiler_params=pltpu.CompilerParams(vmem_limit_bytes=4 * 2**20),
+    )(*(pltpu.with_memory_space_constraint(field, pltpu.VMEM) for field in fields))
 
 
 def solution(mesh):

time: 83.4 us -> 81.9 us (0.982)
  the two profiles are of different devices: /device:TPU:135 before, /device:TPU:193 now
where the time goes in v4:
time: 81.9 us; the launch traced here: 81.8 us
  Pallas kernels  81.2 us (99%)
    pallas_call x1, Pallas kernels, shards(): pl.pallas_call(kernel, out_shape=[pltpu.VMEM(part, F32) for part in parts...  79.1 us
    pallas_call x1, Pallas kernels, shards(): pl.pallas_call(finish, out_shape=(grid, grid), in_specs=[vmem] * len(part...  2.1 us

profile of v4, /device:TPU:193, one launch (start us, length us, event | category | flops | bytes accessed | tf_op | source)
XLA Modules:
  0.0 81.8 jit_solution(16414021469036629994)
XLA Ops:
  0.6 79.1 %shard_map.131 = (f32[3,8,16,512]{3,2,1,0:T(8,128)S(1)}, f32[3,11,16,512]{3,2,1,0:T(8,128)S(1)}, f32[3,16,512]{2,1,0:T(8,128)S(1)}, f32[3,24,512]{2,1,0:T(8,128)...) custom-call(f32[3,8,16,512]{3,2,1,0:T(8,128)} %disp_hbm.1, ...), custom_call_target="tpu_custom_call" | custom-call | tf_op jit(solution)/shard_map/pallas_call | solution.py:638
  79.7 2.1 %shard_map.132 = (f32[3,8,16,512]{3,2,1,0:T(8,128)}, f32[3,8,16,512]{3,2,1,0:T(8,128)}) custom-call(f32[3,8,16,512]{3,2,1,0:T(8,128)S(1)} %get-tuple-element.11.regrid_ref, f32[3,11,16,512]{3,2,1,0:T(8,128)S(1)} %get-tuple-element.12.spd, f32[3,16,512]{2,1,0:T(8,128)S(1)} %get-tuple-element.13.xm1, f32[3,24,512]{2,1,0:T(8,128)S(1)} %get-tuple-element.14.xp16, ...), custom_call_target="tpu_custom_call" | custom-call | tf_op jit(solution)/shard_map/pallas_call | solution.py:719

commit v5 on v4

--- a/solution.py
+++ b/solution.py
@@ -69,7 +69,7 @@
 def kernel(
     disp_hbm, mass_hbm, mom_hbm, frac_hbm, order_hbm, owner_hbm, block_hbm,
     kmass_hbm, kmom_hbm, panels_hbm, pids_hbm, flags_hbm,
-    regrid_ref, spd, xm1, xp16, side, visc, pres, dens, trac,
+    regrid_ref, spd, xm1, xp16, side, visc, pres, dens, trac, vel,
     order_ref, owner_ref, block_ref, panels_ref, pids_ref, flags_ref,
     ext, s1, old, frac, kmass, kmom, vol, sel_src, table, send, mid, recv, ids_send, ids_mid, ids_recv,
     sel_dst, xst, xhl, xhr, cst, chl, pans, plane, qst, xq, crs, crn,
@@ -256,7 +256,7 @@
     class Shift:
         def __init__(self, src, dst, ssem, rsem, dz, dx):
             self.copy = remote(src, dst, ssem, rsem, neighbour(dz, dx))
-            self.goes, self.comes = there(dz, dx), there(-dz, -dx)
+            self.goes, self.comes, self.flat = there(dz, dx), there(-dz, -dx), dz == 0
 
         def start(self):
             pl.when(self.goes)(self.copy.start)
@@ -498,15 +498,68 @@
         div = div + (here - behind_y(here))
         pres[z] = -penalty_factor * div
 
-    lax.fori_loop(1, CZ, lambda i, carry: (viscosity(i, None), carry)[1], 0)
+    lax.fori_loop(1, CZ, lambda i, carry: (viscosity(i, None), carry)[1], 0, unroll=7)
     lax.fori_loop(1, CZ, lambda z, carry: (pressure(z, None), carry)[1], 0)
 
+    def x_ends():
+        @pl.when(at_left)
+        def _():
+            for c in range(3):
+                xm1[c] = jnp.zeros((16, CY), F32)
+
+        @pl.when(at_right)
+        def _():
+            for c in range(3):
+                xp16[c] = jnp.zeros((24, CY), F32)
+
+    def lines(final):
+        squares_m = jnp.zeros((CZ, CY), F32)
+        squares_l = jnp.zeros((CZ, CY), F32)
+        squares_p = xq[...]
+        for c in range(3):
+            whole = xm1[c]
+            here = whole[0:8]
+            above = pltpu.roll(whole, 15, 0)[0:8]
+            squares_m = squares_m + squared(here, above, plane[c, 0:8, :], ahead_y(here))
+            whole = xp16[c]
+            here = whole[8:16]
+            above = pltpu.roll(whole, 23, 0)[8:16]
+            squares_p = squares_p + squared(here, above, ahead_y(here))
+            last = plane[c, 8:16, :]
+            above = ahead_x(last, spd[c, 1 + CZ, CX - 1 : CX, :] if final else last)
+            squares_l = squares_l + squared(last, above, here, ahead_y(last))
+        side[0:8, :] = jnp.where(at_left, 0.0, visc_of(squares_m))
+        side[8:16, :] = jnp.where(at_right, 0.0, visc_of(squares_p))
+        here = xp16[0]
+        div = here[8:16] - pltpu.roll(here, 1, 0)[8:16]
+        div = div + (xp16[1, 8:16, :] - plane[1, 8:16, :])
+        here = xp16[2, 8:16, :]
+        div = div + (here - behind_y(here))
+        side[16:24, :] = jnp.where(at_right, 0.0, -penalty_factor * div)
+        here = plane[0, 0:8, :]
+        div = here - behind_x(here, spd[0, 0, 0:1, :] if final else here)
+        div = div + (plane[1, 0:8, :] - xm1[1, 0:8, :])
+        here = plane[2, 0:8, :]
+        div = div + (here - behind_y(here))
+        visc[1 : 1 + CZ, CX - 1, :] = visc_of(squares_l)
+        pres[0:CZ, 0, :] = -penalty_factor * div
+
     for copy in spd_copies:
-        copy.wait()
+        if copy.flat:
+            copy.wait()
+    x_ends()
+    lines(False)
+    for z in range(1, CZ - 2):
+        update(z, vel, spd, xm1, xp16, side, visc, pres, dens, trac)
+
+    for copy in spd_copies:
+        if not copy.flat:
+            copy.wait()
     for c in range(3):
         xm1[c, 8:9, :] = crn[0, c]
         xp16[c, 7:8, :] = crn[1, c]
         xp16[c, 16:17, :] = crn[2, c]
+    x_ends()
 
     @pl.when(at_bottom)
     def _():
@@ -521,52 +574,12 @@
             xm1[c, 8:16, :] = nothing
             xp16[c, 16:24, :] = nothing
 
-    @pl.when(at_left)
-    def _():
-        for c in range(3):
-            xm1[c] = jnp.zeros((16, CY), F32)
-
-    @pl.when(at_right)
-    def _():
-        for c in range(3):
-            xp16[c] = jnp.zeros((24, CY), F32)
-
-    squares_m = jnp.zeros((CZ, CY), F32)
-    squares_l = jnp.zeros((CZ, CY), F32)
-    squares_p = xq[...]
-    for c in range(3):
-        whole = xm1[c]
-        here = whole[0:8]
-        above = pltpu.roll(whole, 15, 0)[0:8]
-        squares_m = squares_m + squared(here, above, plane[c, 0:8, :], ahead_y(here))
-        whole = xp16[c]
-        here = whole[8:16]
-        above = pltpu.roll(whole, 23, 0)[8:16]
-        squares_p = squares_p + squared(here, above, ahead_y(here))
-        last = plane[c, 8:16, :]
-        above = ahead_x(last, spd[c, 1 + CZ, CX - 1 : CX, :])
-        squares_l = squares_l + squared(last, above, here, ahead_y(last))
-    side[0:8, :] = jnp.where(at_left, 0.0, visc_of(squares_m))
-    side[8:16, :] = jnp.where(at_right, 0.0, visc_of(squares_p))
-    here = xp16[0]
-    div = here[8:16] - pltpu.roll(here, 1, 0)[8:16]
-    div = div + (xp16[1, 8:16, :] - plane[1, 8:16, :])
-    here = xp16[2, 8:16, :]
-    div = div + (here - behind_y(here))
-    side[16:24, :] = jnp.where(at_right, 0.0, -penalty_factor * div)
-    here = plane[0, 0:8, :]
-    div = here - behind_x(here, spd[0, 0, 0:1, :])
-    div = div + (plane[1, 0:8, :] - xm1[1, 0:8, :])
-    here = plane[2, 0:8, :]
-    div = div + (here - behind_y(here))
-
     viscosity(0, 7)
     viscosity(CZ, 15)
     viscosity(CZ + 1, 16)
     pressure(0, 0)
     pressure(CZ, 8)
-    visc[1 : 1 + CZ, CX - 1, :] = visc_of(squares_l)
-    pres[0:CZ, 0, :] = -penalty_factor * div
+    lines(True)
 
     @pl.when(at_bottom)
     def _():
@@ -585,36 +598,41 @@
     regrid_out.wait()
 
 
-def finish(regrid_ref, spd, xm1, xp16, side, visc, pres, dens, trac, regrid_hbm, vel_hbm, vel, sem):
-    regrid_out = pltpu.make_async_copy(regrid_ref, regrid_hbm, sem.at[CZ])
-    regrid_out.start()
-
-    def update(z, carry):
-        v = visc[z + 1]
-        line = pl.ds(z, 1)
-        v_next = (visc[z + 2], ahead_x(v, side[pl.ds(z + 8, 1), :]), ahead_y(v))
-        v_prev = (visc[z], behind_x(v, side[line, :]), behind_y(v))
-        forward = [0.5 * (v + other) for other in v_next]
-        backward = [0.5 * (v + other) for other in v_prev]
-        density = dens[z]
-        bottom = forward[0] + backward[0] + forward[1] + backward[1] + forward[2] + backward[2] + density
-        p = pres[z]
-        p_next = (pres[z + 1], ahead_x(p, side[pl.ds(z + 16, 1), :]), ahead_y(p))
-        for c in range(3):
-            here = spd[c, z + 1]
-            top = forward[0] * spd[c, z + 2] + backward[0] * spd[c, z]
-            top = top + forward[1] * ahead_x(here, xp16[c, pl.ds(z + 8, 1), :])
-            top = top + backward[1] * behind_x(here, xm1[c, line, :])
-            top = top + forward[2] * ahead_y(here) + backward[2] * behind_y(here)
-            top = top - (p_next[c] - p) + trac[c] + density * here
-            vel[c, z] = top / bottom
-        pltpu.make_async_copy(vel.at[:, z], vel_hbm.at[:, z], sem.at[z]).start()
-        return carry
-
-    lax.fori_loop(0, CZ, update, 0)
-    for z in range(CZ):
-        pltpu.make_async_copy(vel.at[:, z], vel_hbm.at[:, z], sem.at[z]).wait()
-    regrid_out.wait()
+def update(z, vel, spd, xm1, xp16, side, visc, pres, dens, trac):
+    v = visc[z + 1]
+    line = pl.ds(z, 1)
+    v_next = (visc[z + 2], ahead_x(v, side[pl.ds(z + 8, 1), :]), ahead_y(v))
+    v_prev = (visc[z], behind_x(v, side[line, :]), behind_y(v))
+    forward = [0.5 * (v + other) for other in v_next]
+    backward = [0.5 * (v + other) for other in v_prev]
+    density = dens[z]
+    bottom = forward[0] + backward[0] + forward[1] + backward[1] + forward[2] + backward[2] + density
+    p = pres[z]
+    p_next = (pres[z + 1], ahead_x(p, side[pl.ds(z + 16, 1), :]), ahead_y(p))
+    for c in range(3):
+        here = spd[c, z + 1]
+        top = forward[0] * spd[c, z + 2] + backward[0] * spd[c, z]
+        top = top + forward[1] * ahead_x(here, xp16[c, pl.ds(z + 8, 1), :])
+        top = top + backward[1] * behind_x(here, xm1[c, line, :])
+        top = top + forward[2] * ahead_y(here) + backward[2] * behind_y(here)
+        top = top - (p_next[c] - p) + trac[c] + density * here
+        vel[c, z] = top / bottom
+
+
+def finish(regrid_ref, spd, xm1, xp16, side, visc, pres, dens, trac, vel, regrid_hbm, vel_hbm, late, sem):
+    early = pl.ds(1, CZ - 3)
+    copies = [
+        pltpu.make_async_copy(vel.at[:, early], vel_hbm.at[:, early], sem.at[CZ]),
+        pltpu.make_async_copy(regrid_ref, regrid_hbm, sem.at[CZ + 1]),
+    ]
+    for copy in copies:
+        copy.start()
+    for z in (0, CZ - 2, CZ - 1):
+        update(z, late, spd, xm1, xp16, side, visc, pres, dens, trac)
+        copies.append(pltpu.make_async_copy(late.at[:, z], vel_hbm.at[:, z], sem.at[z]))
+        copies[-1].start()
+    for copy in copies:
+        copy.wait()
 
 
 def shards(
@@ -634,6 +652,7 @@
         (CZ + 1, CX, CY),
         (CZ, CX, CY),
         (3, CX, CY),
+        grid.shape,
     )
     fields = pl.pallas_call(
         kernel,
@@ -721,7 +740,7 @@
         out_shape=(grid, grid),
         in_specs=[vmem] * len(parts),
         out_specs=(hbm, hbm),
-        scratch_shapes=[pltpu.VMEM(grid.shape, F32), dma((CZ + 1,))],
+        scratch_shapes=[pltpu.VMEM(grid.shape, F32), dma((CZ + 2,))],
         compiler_params=pltpu.CompilerParams(vmem_limit_bytes=4 * 2**20),
     )(*(pltpu.with_memory_space_constraint(field, pltpu.VMEM) for field in fields))
 

time: 81.9 us -> 81 us (0.989)
  Pallas kernels: 81.2 us -> 80.3 us
    pallas_call x1, Pallas kernels: 2.1 us -> 1.23 us  [shards(): pl.pallas_call(finish, out_shape=(grid, grid), in_specs=[vmem] * len(part...]
where the time goes in v5:
time: 81 us; the launch traced here: 80.9 us
  Pallas kernels  80.3 us (99%)
    pallas_call x1, Pallas kernels, shards(): pl.pallas_call(kernel, out_shape=[pltpu.VMEM(part, F32) for part in parts...  79 us

profile of v5, /device:TPU:193, one launch (start us, length us, event | category | flops | bytes accessed | tf_op | source)
XLA Modules:
  0.0 80.9 jit_solution(8803958369929690093)
XLA Ops:
  0.6 79.0 %shard_map.131 = (f32[3,8,16,512]{3,2,1,0:T(8,128)S(1)}, f32[3,11,16,512]{3,2,1,0:T(8,128)S(1)}, f32[3,16,512]{2,1,0:T(8,128)S(1)}, f32[3,24,512]{2,1,0:T(8,128)...) custom-call(f32[3,8,16,512]{3,2,1,0:T(8,128)} %disp_hbm.1, ...), custom_call_target="tpu_custom_call" | custom-call | tf_op jit(solution)/shard_map/pallas_call | solution.py:657
  79.7 1.2 %shard_map.132 = (f32[3,8,16,512]{3,2,1,0:T(8,128)}, f32[3,8,16,512]{3,2,1,0:T(8,128)}) custom-call(f32[3,8,16,512]{3,2,1,0:T(8,128)S(1)} %get-tuple-element.12.regrid_ref, f32[3,11,16,512]{3,2,1,0:T(8,128)S(1)} %get-tuple-element.13.spd, f32[3,16,512]{2,1,0:T(8,128)S(1)} %get-tuple-element.14.xm1, f32[3,24,512]{2,1,0:T(8,128)S(1)} %get-tuple-element.15.xp16, ...), custom_call_target="tpu_custom_call" | custom-call | tf_op jit(solution)/shard_map/pallas_call | solution.py:738
